TPU v7x, 32 devices: a whole 2x2x4 slice. The times are simulated.
32 devices in a mesh: section: 2 (over core), batch: 16 (over z, y, x).
Axes of the slice: x: 2, y: 2, z: 4, core: 2. Of those that a mesh axis runs over, the one named last changes fastest.
Arguments:
- inputs: bfloat16 [2, 16, 64, 768], P(None, 'batch'), may hold values from -6 to 6
- cotangent: bfloat16 [2, 16, 64, 768], P(None, 'batch'), may hold values from -6 to 6
- segments: int32 [2, 16, 64], P(None, 'batch'), may hold values from 0 to 3, never falling along the last dimension, each value on 1 to 32 neighbouring positions
- row_widths: int32 [2, 16, 4], P(None, 'batch'), may hold values from 4 to 16
- w_qkv: bfloat16 [2, 768, 2304], P('section'), may hold values from -0.21875 to 0.21875
- w_out: bfloat16 [2, 768, 768], P('section'), may hold values from -0.625 to 0.625
- w_fc1: bfloat16 [2, 768, 3072], P('section'), may hold values from -0.21875 to 0.21875
- w_fc2: bfloat16 [2, 3072, 768], P('section'), may hold values from -0.109375 to 0.109375
- norm_gains: float32 [2, 4, 768], P('section'), may hold values from 0.25 to 1.75
- bias_rows: float32 [2, 6, 768], P('section'), may hold values from -4 to 4
- fc1_bias: float32 [2, 3072], P('section'), may hold values from -4 to 4
- rel_table: float32 [2, 12, 729], P('section'), may hold values from -6 to 6
Outputs:
- activations: bfloat16 [2, 2, 16, 64, 768], P('section', None, 'batch')
- input_grads: float32 [2, 2, 16, 64, 768], P('section', None, 'batch')
- grad_qkv: float32 [2, 768, 2304], P('section', 'batch')
- grad_out: float32 [2, 768, 768], P('section', 'batch')
- grad_fc1: float32 [2, 768, 3072], P('section', 'batch')
- grad_fc2: float32 [2, 3072, 768], P('section', 'batch')
- grad_gains: float32 [2, 4, 768], P('section')
- grad_biases: float32 [2, 6, 768], P('section')
- grad_fc1_bias: float32 [2, 3072], P('section')
- grad_table: float32 [2, 12, 729], P('section')
Inputs may be any that keep to these rules, and one draw needn't show every extreme that they name: `segments`: along a packed row the numbers never fall and each of the 4 images has 1 to 32 slots; every image number occurs in every row.
All inputs are finite; a program needn't handle non-finite values.
Results may differ from a plain program's by a relative error of at most 0.02.
Values may be sent and summed in bfloat16 or wider, within the bound.
A program may use at most 256 MiB of HBM per device.

v0:
```python
import jax
import jax.numpy as jnp
from jax import lax
from jax.sharding import PartitionSpec as P

REACH = 13


NORM_EPS = 1e-06
ROOT_HALF = 0.7071067811865476
INV_ROOT_TWO_PI = 0.3989422804014327


def passed_along(value, axis, steps):
    count = lax.axis_size(axis)
    leading, last = (max(0, -steps), min(count, count - steps))
    return lax.ppermute(value, axis, [(source, source + steps) for source in range(leading, last)])


def norm_parts(values_in):
    row_mean = jnp.mean(values_in, axis=-1, keepdims=True)
    centered = values_in - row_mean
    inv_scale = lax.rsqrt(jnp.mean(centered * centered, axis=-1, keepdims=True) + NORM_EPS)
    return (centered * inv_scale, inv_scale)


def norm_back(upstream, normal_in, inv_scale):
    return inv_scale * (
        upstream
        - jnp.mean(upstream, axis=-1, keepdims=True)
        - normal_in * jnp.mean(upstream * normal_in, axis=-1, keepdims=True)
    )


def geometry(segment_row, width_row):
    slot_ids = jnp.arange(segment_row.shape[0], dtype=jnp.int32)
    same_image = segment_row[:, None] == segment_row[None, :]
    before = jnp.sum((segment_row[None, :] < segment_row[:, None]).astype(jnp.int32), axis=1)
    place_in = slot_ids - before
    one_hot = (
        segment_row[:, None] == jnp.arange(width_row.shape[0], dtype=jnp.int32)[None, :]
    ).astype(jnp.int32)
    img_width = jnp.sum(one_hot * width_row[None, :], axis=1)
    grid_row = place_in // img_width
    column = place_in % img_width
    row_step = jnp.clip(grid_row[:, None] - grid_row[None, :], -REACH, REACH) + REACH
    col_step = jnp.clip(column[:, None] - column[None, :], -REACH, REACH) + REACH
    rel_index = row_step * (2 * REACH + 1) + col_step
    return (same_image, rel_index)


def forward(layer_in, weights, same_image, rel_index):
    w_qkv, w_out, w_fc1, w_fc2, norm_gains, bias_rows, fc1_bias, pos_table = weights
    slot_count, model_width = layer_in.shape
    head_count = pos_table.shape[0]
    head_size = model_width // head_count
    hat_one, scale_one = norm_parts(layer_in)
    normed = (hat_one * norm_gains[0] + bias_rows[0]).astype(jnp.bfloat16)
    qkv_bias = jnp.concatenate([bias_rows[1], jnp.zeros_like(bias_rows[1]), bias_rows[2]])
    qkv_rows = (jnp.dot(normed, w_qkv, preferred_element_type=jnp.float32) + qkv_bias).astype(
        jnp.bfloat16
    )
    qkv_split = qkv_rows.reshape(slot_count, 3, head_count, head_size)
    queries, key_rows, values = (qkv_split[:, 0], qkv_split[:, 1], qkv_split[:, 2])
    raw_scores = jnp.einsum("qhd,khd->hqk", queries, key_rows, preferred_element_type=jnp.float32)
    pos_bias = jnp.take(pos_table, rel_index, axis=1)
    scores = jnp.where(same_image[None], raw_scores * 0.125 + pos_bias, -1e30)
    row_max = jnp.max(scores, axis=-1, keepdims=True)
    exp_scores = jnp.exp(scores - row_max)
    att_probs = exp_scores / jnp.sum(exp_scores, axis=-1, keepdims=True)
    att_low = att_probs.astype(jnp.bfloat16)
    mixed_out = jnp.einsum("hqk,khd->qhd", att_low, values, preferred_element_type=jnp.float32)
    mixed_out = mixed_out.reshape(slot_count, model_width).astype(jnp.bfloat16)
    att_out = jnp.dot(mixed_out, w_out, preferred_element_type=jnp.float32) + bias_rows[3]
    middle = layer_in + norm_gains[1] * att_out
    hat_two, scale_two = norm_parts(middle)
    second = (hat_two * norm_gains[2] + bias_rows[4]).astype(jnp.bfloat16)
    hidden = jnp.dot(second, w_fc1, preferred_element_type=jnp.float32) + fc1_bias
    active = jax.nn.gelu(hidden, approximate=False).astype(jnp.bfloat16)
    branch = jnp.dot(active, w_fc2, preferred_element_type=jnp.float32) + bias_rows[5]
    block_out = middle + norm_gains[3] * branch
    kept_parts = (
        hat_one,
        scale_one,
        normed,
        queries,
        key_rows,
        values,
        att_probs,
        att_low,
        mixed_out,
        att_out,
        hat_two,
        scale_two,
        second,
        hidden,
        active,
        branch,
    )
    return (block_out, kept_parts)


def backward(grad_out, kept_parts, weights, rel_index):
    w_qkv, w_out, w_fc1, w_fc2, norm_gains, bias_rows, fc1_bias, pos_table = weights
    (
        hat_one,
        scale_one,
        normed,
        queries,
        key_rows,
        values,
        att_probs,
        att_low,
        mixed_out,
        att_out,
        hat_two,
        scale_two,
        second,
        hidden,
        active,
        branch,
    ) = kept_parts
    slot_count, model_width = grad_out.shape
    head_count, rel_count = pos_table.shape
    head_size = model_width // head_count
    g_layer_two = jnp.sum(grad_out * branch, axis=0)
    d_branch = (norm_gains[3] * grad_out).astype(jnp.bfloat16)
    g_fc2 = jnp.dot(active.T, d_branch, preferred_element_type=jnp.float32)
    g_fc2_bias = jnp.sum(d_branch.astype(jnp.float32), axis=0)
    d_active = jnp.dot(d_branch, w_fc2.T, preferred_element_type=jnp.float32)
    cumul = 0.5 * (1.0 + lax.erf(hidden * ROOT_HALF))
    density = jnp.exp(-0.5 * hidden * hidden) * INV_ROOT_TWO_PI
    d_hidden = (d_active * (cumul + hidden * density)).astype(jnp.bfloat16)
    g_fc1 = jnp.dot(second.T, d_hidden, preferred_element_type=jnp.float32)
    g_fc1_bias = jnp.sum(d_hidden.astype(jnp.float32), axis=0)
    d_second = jnp.dot(d_hidden, w_fc1.T, preferred_element_type=jnp.float32)
    g_norm_two = jnp.sum(d_second * hat_two, axis=0)
    g_shift_two = jnp.sum(d_second, axis=0)
    d_middle = grad_out + norm_back(d_second * norm_gains[2], hat_two, scale_two)
    g_layer_one = jnp.sum(d_middle * att_out, axis=0)
    d_att_out = (norm_gains[1] * d_middle).astype(jnp.bfloat16)
    g_out = jnp.dot(mixed_out.T, d_att_out, preferred_element_type=jnp.float32)
    g_out_bias = jnp.sum(d_att_out.astype(jnp.float32), axis=0)
    d_mixed = jnp.dot(d_att_out, w_out.T, preferred_element_type=jnp.float32).astype(jnp.bfloat16)
    d_mixed = d_mixed.reshape(slot_count, head_count, head_size)
    d_probs = jnp.einsum("qhd,khd->hqk", d_mixed, values, preferred_element_type=jnp.float32)
    d_value = jnp.einsum("hqk,qhd->khd", att_low, d_mixed, preferred_element_type=jnp.float32)
    d_scores = att_probs * (d_probs - jnp.sum(att_probs * d_probs, axis=-1, keepdims=True))
    flat_index = rel_index.reshape(-1)
    g_table = jax.vmap(
        lambda head_vals: jax.ops.segment_sum(head_vals, flat_index, num_segments=rel_count)
    )(d_scores.reshape(head_count, -1))
    d_raw = (0.125 * d_scores).astype(jnp.bfloat16)
    d_query = jnp.einsum("hqk,khd->qhd", d_raw, key_rows, preferred_element_type=jnp.float32)
    d_key = jnp.einsum("hqk,qhd->khd", d_raw, queries, preferred_element_type=jnp.float32)
    d_qkv = (
        jnp.stack([d_query, d_key, d_value], axis=1)
        .reshape(slot_count, 3 * model_width)
        .astype(jnp.bfloat16)
    )
    g_qkv = jnp.dot(normed.T, d_qkv, preferred_element_type=jnp.float32)
    d_qkv_wide = d_qkv.astype(jnp.float32)
    g_query_bias = jnp.sum(d_qkv_wide[:, :model_width], axis=0)
    g_value_bias = jnp.sum(d_qkv_wide[:, 2 * model_width :], axis=0)
    d_normed = jnp.dot(d_qkv, w_qkv.T, preferred_element_type=jnp.float32)
    g_norm_one = jnp.sum(d_normed * hat_one, axis=0)
    g_shift_one = jnp.sum(d_normed, axis=0)
    d_layer_in = d_middle + norm_back(d_normed * norm_gains[0], hat_one, scale_one)
    g_gains = jnp.stack([g_norm_one, g_layer_one, g_norm_two, g_layer_two])
    g_shifts = jnp.stack(
        [g_shift_one, g_query_bias, g_value_bias, g_out_bias, g_shift_two, g_fc2_bias]
    )
    return (d_layer_in, (g_qkv, g_out, g_fc1, g_fc2, g_gains, g_shifts, g_fc1_bias, g_table))


def per_device(
    inputs,
    cotangent,
    segments,
    row_widths,
    w_qkv,
    w_out,
    w_fc1,
    w_fc2,
    norm_gains,
    bias_rows,
    fc1_bias,
    rel_table,
):
    section_zero = lax.axis_index("section") == 0
    micro_count = inputs.shape[0]
    slot_count = inputs.shape[2]
    model_width = inputs.shape[3]
    weights = (
        w_qkv[0],
        w_out[0],
        w_fc1[0],
        w_fc2[0],
        norm_gains[0],
        bias_rows[0],
        fc1_bias[0],
        rel_table[0],
    )
    layouts = [
        geometry(segments[micro_no, 0], row_widths[micro_no, 0]) for micro_no in range(micro_count)
    ]

    def choose(left_tree, right_tree):
        return jax.tree.map(
            lambda left_val, right_val: jnp.where(section_zero, left_val, right_val),
            left_tree,
            right_tree,
        )

    arriving = jnp.zeros((slot_count, model_width), jnp.bfloat16)
    entered = []
    produced = []
    for step_no in range(micro_count + 1):
        fwd_micro = min(step_no, micro_count - 1)
        prev_micro = max(step_no - 1, 0)
        same_image, rel_index = choose(layouts[fwd_micro], layouts[prev_micro])
        entering = jnp.where(section_zero, inputs[fwd_micro, 0], arriving)
        active_flag = jnp.where(section_zero, step_no < micro_count, step_no >= 1)

        def advance(packed):
            return forward(packed[0].astype(jnp.float32), weights, packed[1], packed[2])[0]

        def pause(packed):
            return jnp.zeros((slot_count, model_width), jnp.float32)

        layer_out = lax.cond(active_flag, advance, pause, (entering, same_image, rel_index))
        layer_out = layer_out.astype(jnp.bfloat16)
        entered.append(entering)
        produced.append(layer_out)
        if step_no < micro_count:
            arriving = passed_along(layer_out, "section", 1)
    returned = jnp.zeros((slot_count, model_width), jnp.bfloat16)
    leaving = []
    totals = tuple((jnp.zeros(weight.shape, jnp.float32) for weight in weights))
    big_parts = None
    for step_no in range(micro_count + 1):
        last_micro = min(step_no, micro_count - 1)
        early_micro = max(step_no - 1, 0)
        same_image, rel_index = choose(layouts[early_micro], layouts[last_micro])
        grad_out = jnp.where(section_zero, returned, cotangent[last_micro, 0]).astype(jnp.float32)
        active_flag = jnp.where(section_zero, step_no >= 1, step_no < micro_count)
        carried = totals
        skip_count = 8 - len(carried)

        def fold_in(local_grads, running):
            big_local = local_grads[:skip_count]
            rest = tuple(
                (
                    left_val + right_val
                    for left_val, right_val in zip(running, local_grads[skip_count:])
                )
            )
            return (big_local, rest)

        entering = choose(entered[early_micro], entered[last_micro + 1])

        def retreat(packed):
            kept_again = forward(packed[1].astype(jnp.float32), weights, packed[2], packed[3])[1]
            grad_in, local_grads = backward(packed[0], kept_again, weights, packed[3])
            return (grad_in,) + fold_in(local_grads, packed[4])

        operands = (grad_out, entering, same_image, rel_index, carried)

        def spare_fn(packed):
            big_zero = tuple(
                (jnp.zeros(weights[slot_no].shape, jnp.float32) for slot_no in range(skip_count))
            )
            return (jnp.zeros((slot_count, model_width), jnp.float32), big_zero, packed[-1])

        grad_in, big_local, carried = lax.cond(active_flag, retreat, spare_fn, operands)
        leaving.append(grad_in)
        totals = carried
        if step_no < micro_count:
            returned = passed_along(grad_in.astype(jnp.bfloat16), "section", -1)
    big_parts = (
        lax.psum_scatter(totals[0], "batch", scatter_dimension=0, tiled=True),
        lax.psum_scatter(totals[1], "batch", scatter_dimension=0, tiled=True),
        lax.psum_scatter(totals[2], "batch", scatter_dimension=0, tiled=True),
        lax.psum_scatter(totals[3], "batch", scatter_dimension=0, tiled=True),
    )
    small_parts = lax.psum((totals[4], totals[5], totals[6], totals[7]), "batch")
    activations = jnp.stack(
        [
            jnp.where(section_zero, produced[micro_no], produced[micro_no + 1])
            for micro_no in range(micro_count)
        ]
    )[None, :, None]
    input_grads = jnp.stack(
        [
            jnp.where(section_zero, leaving[micro_no + 1], leaving[micro_no])
            for micro_no in range(micro_count)
        ]
    )[None, :, None]
    return (
        activations,
        input_grads,
        big_parts[0][None],
        big_parts[1][None],
        big_parts[2][None],
        big_parts[3][None],
        small_parts[0][None],
        small_parts[1][None],
        small_parts[2][None],
        small_parts[3][None],
    )


def solution(mesh):
    return jax.shard_map(
        per_device,
        mesh=mesh,
        in_specs=(
            P(None, "batch", None, None),
            P(None, "batch", None, None),
            P(None, "batch", None),
            P(None, "batch", None),
            P("section", None, None),
            P("section", None, None),
            P("section", None, None),
            P("section", None, None),
            P("section", None, None),
            P("section", None, None),
            P("section", None),
            P("section", None, None),
        ),
        out_specs=(
            P("section", None, "batch", None, None),
            P("section", None, "batch", None, None),
            P("section", "batch", None),
            P("section", "batch", None),
            P("section", "batch", None),
            P("section", "batch", None),
            P("section", None, None),
            P("section", None, None),
            P("section", None),
            P("section", None, None),
        ),
        check_vma=False,
    )
```

profile of v0, /device:TPU:0, one launch (start us, length us, event | category | flops | bytes accessed | tf_op | source)
XLA Modules:
  0.0 1178.7 jit_solution(13244365912392746714)
XLA Ops:
  13.4 31.7 %conditional.4 = (bf16[64,768]{1,0:T(8,128)(2,1)S(1)}) conditional(s32[]{:T(128)} %convert_element_type.339, () %tuple.47, (bf16[64,768]{1,0:T(8,128)(2,1)S(1)}, f32[4,768]{1,0:T(4,128)}, f32[6,768]{1,0:T(8,128)S(1)}, bf16[768,2304]{1,0:T(8,128)(2,1)}, pred[64,64]{1,0:T(8,128)(4,1)}, /*index=5*/f32[12,729]{0,1:T(8,128)S(1)}, s32[64,64]{1,0:T(8,128)S(1)}, ...), branch_computations={%region_2.3_spmd, %region_3.11_spmd} | conditional | flops 933787136 | bytes 24433248 | solution.py:231
  14.7 2.8 fusion.1
  19.1 14.1 %gather_fusion = f32[4096,12]{1,0:T(8,128)} fusion(f32[12,729]{0,1:T(8,128)S(1)} %get-tuple-element.221, s32[4096]{0:T(1024)S(1)} %broadcast_clamp_fusion), kind=kCustom, calls=%fused_computation.clone | custom fusion | bytes 409600 | tf_op jit(solution)/shard_map/cond/branch_1_fun/jit(_take)/gather | solution.py:66
  33.2 2.8 copy.161
  38.2 6.9 fusion.10
  49.3 14.1 %gather_fusion.4 = f32[4096,12]{1,0:T(8,128)} fusion(f32[12,729]{0,1:T(8,128)S(1)} %bitcast.336, s32[4096]{0:T(1024)S(1)} %broadcast_clamp_fusion.5), kind=kCustom, calls=%fused_computation.4.clone | custom fusion | bytes 409600 | tf_op jit(solution)/shard_map/cond/branch_1_fun/jit(_take)/gather | solution.py:66
  63.4 2.7 copy.213
  66.7 2.8 fusion.321
  73.6 7.5 fusion.336
  81.1 2.1 collective-permute-start.1
  83.2 14.1 %gather_fusion.5 = f32[4096,12]{1,0:T(8,128)} fusion(f32[12,729]{0,1:T(8,128)S(1)} %bitcast.337, s32[4096]{0:T(1024)S(1)} %broadcast_clamp_fusion.4), kind=kCustom, calls=%fused_computation.5.clone | custom fusion | bytes 409600 | tf_op jit(solution)/shard_map/cond/branch_1_fun/jit(_take)/gather | solution.py:66
  97.3 3.4 copy.223
  102.8 24.1 %conditional.6 = (f32[64,768]{1,0:T(8,128)S(1)}, f32[768,2304]{1,0:T(8,128)}, f32[768,768]{1,0:T(8,128)}, f32[768,3072]{1,0:T(8,128)}, f32[3072,768]{1,0:T(8,128...) conditional(s32[]{:T(128)} %convert_element_type.352, () %tuple.51, ...), branch_computations={%region_26.28_spmd, %region_27.52_spmd} | conditional | flops 2790748160 | bytes 130560736 | solution.py:275
  102.8 3.3 broadcast_in_dim.120
  107.7 4.8 broadcast_in_dim.122
  112.6 4.2 broadcast_in_dim.123
  130.3 2.8 fusion.322
  143.8 3.5 convolution_add_fusion.22
  147.4 49.0 %collective-permute-done.2 = bf16[64,768]{1,0:T(8,128)(2,1)} collective-permute-done((bf16[64,768]{1,0:T(8,128)(2,1)}, bf16[64,768]{1,0:T(8,128)(2,1)}, u32[]{:S(2)}, u32[]{:S(2)}) %collective-permute-start.2) | collective-permute-done | bytes 98336 | tf_op jit(solution)/shard_map/ppermute | solution.py:17
  197.9 4.5 convert_reduce_fusion.10
  202.4 2.2 multiply_reduce_fusion.17
  207.3 2.1 convolution_bitcast_fusion
  216.4 5.1 fusion.490
  221.5 6.7 fusion.435
  228.3 2.7 fusion.337
  231.2 4.1 fusion.487
  247.0 8.9 add.775
  255.9 3.3 add.776
  259.2 12.9 %add.777 = f32[768,3072]{1,0:T(8,128)} add(f32[768,3072]{1,0:T(8,128)} %get-tuple-element.313, f32[768,3072]{1,0:T(8,128)} %fusion.490) | non-fusion elementwise | flops 2359296 | bytes 28311552 | tf_op jit(solution)/shard_map/cond/branch_1_fun/add | solution.py:254
  272.1 11.4 add.778
  285.4 22.8 %scatter_fusion.1 = f32[12,729]{0,1:T(8,128)S(1)} fusion(f32[12,729]{0,1:T(8,128)S(1)} %get-tuple-element.318, s32[4096]{0:T(1024)S(1)} %copy-done.84, f32[4096,12]{1,0:T(8,128)} %copy.234), kind=kCustom, calls=%fused_computation.8 | custom fusion | flops 49152 | bytes 606208 | tf_op jit(solution)/shard_map/cond/branch_1_fun/vmap()/scatter-add | solution.py:151
  308.3 106.1 %conditional.7 = (f32[64,768]{1,0:T(8,128)}, f32[768,2304]{1,0:T(8,128)}, f32[768,768]{1,0:T(8,128)}, f32[768,3072]{1,0:T(8,128)}, f32[3072,768]{1,0:T(8,128)}, ...) conditional(s32[]{:T(128)} %convert_element_type.339, ...), branch_computations={%region_74.76_spmd, %region_75.100_spmd} | conditional | flops 2797345280 | bytes 312253568 | solution.py:275
  311.1 2.8 fusion.269
  319.4 14.2 %gather_fusion.3 = f32[4096,12]{1,0:T(8,128)} fusion(f32[12,729]{0,1:T(8,128)S(1)} %get-tuple-element.268, s32[4096]{0:T(1024)S(1)} %broadcast_clamp_fusion.3), kind=kCustom, calls=%fused_computation.3.clone | custom fusion | bytes 409600 | tf_op jit(solution)/shard_map/cond/branch_1_fun/jit(_take)/gather | solution.py:66
  333.6 3.4 copy.192
  342.3 3.4 convolution_add_fusion.16
  345.7 4.2 convert_reduce_fusion.6
  350.0 2.2 multiply_reduce_fusion.10
  353.7 2.0 fusion.276
  363.3 8.0 convolution_add_fusion.12
  376.2 4.6 convolution_add_fusion.13
  381.0 2.3 fusion.278
  391.4 22.8 %scatter_fusion = f32[12,729]{0,1:T(8,128)S(1)} fusion(f32[12,729]{0,1:T(8,128)S(1)} %get-tuple-element.281, s32[4096]{0:T(1024)S(1)} %reshape.682, f32[4096,12]{1,0:T(8,128)} %copy.203), kind=kCustom, calls=%fused_computation.7 | custom fusion | flops 49152 | bytes 606208 | tf_op jit(solution)/shard_map/cond/branch_1_fun/vmap()/scatter-add | solution.py:151
  424.6 99.9 %all-reduce.3.cloned.1.call-done = (f32[1,4,768]{2,1,0:T(4,128)}, f32[1,6,768]{2,0,1:T(1,128)}, f32[1,3072]{1,0:T(1,128)}, f32[1,12,729]{2,0,1:T(1,128)}) async-done(((f32[1,4,768]{2,1,0:T(4,128)}, f32[1,6,768]{2,0,1:T(1,128)}, f32[1,3072]{1,0:T(1,128)}, f32[1,12,729]{2,0,1:T(1,128)}), (f32[1,4,768]{2,1,0:T(4,128)}, f32[1,6,768]{2,0,1:T(1,128)}, f32[1,3072]{1,0:T(1,128)}, ...) | async-done | bytes 78016 | tf_op jit(solution)/shard_map/psum | solution.py:286
  524.5 133.1 %reduce-scatter.7.cloned.1.call-done = f32[48,768]{1,0:T(8,128)} async-done(((f32[768,768]{1,0:T(8,128)}), f32[48,768]{1,0:T(8,128)}) %reduce-scatter.7.cloned.1.call-update) | async-done | bytes 147472 | tf_op jit(solution)/shard_map/reduce_scatter | solution.py:282
  657.6 156.5 %reduce-scatter.5.cloned.1.call-done = f32[48,2304]{1,0:T(8,128)} async-done(((f32[768,2304]{1,0:T(8,128)}), f32[48,2304]{1,0:T(8,128)}) %reduce-scatter.5.cloned.1.call-update) | async-done | bytes 442384 | tf_op jit(solution)/shard_map/reduce_scatter | solution.py:281
  814.1 176.1 %reduce-scatter.9.cloned.1.call-done = f32[48,3072]{1,0:T(8,128)} async-done(((f32[768,3072]{1,0:T(8,128)}), f32[48,3072]{1,0:T(8,128)}) %reduce-scatter.9.cloned.1.call-update) | async-done | bytes 589840 | tf_op jit(solution)/shard_map/reduce_scatter | solution.py:283
  990.2 176.3 %reduce-scatter.11.cloned.1.call-done = f32[192,768]{1,0:T(8,128)} async-done(((f32[3072,768]{1,0:T(8,128)}), f32[192,768]{1,0:T(8,128)}) %reduce-scatter.11.cloned.1.call-update) | async-done | bytes 589840 | tf_op jit(solution)/shard_map/reduce_scatter | solution.py:284
  (473 shorter events, 113.9 us)
Async XLA Ops:
  7.2 517.3 %all-reduce.3.cloned.1.call-start = ((), (), s32[]{:S(2)}) async-start(), calls=%async_computation.8 | async-start | bytes 159744 | tf_op jit(solution)/shard_map/psum | solution.py:286
  9.7 93.1 %copy-start.51 = (f32[1,6,768]{2,1,0:T(8,128)}, f32[1,6,768]{2,1,0:T(8,128)S(1)}, u32[]{:S(2)}) copy-start(f32[1,6,768]{2,1,0:T(8,128)S(1)} %copy.328) | copy-start | bytes 55300
  13.4 33.3 %copy-start.81 = (f32[1,6,768]{2,0,1:T(1,128)S(1)}, f32[1,6,768]{2,0,1:T(1,128)}, u32[]{:S(2)}) copy-start(f32[1,6,768]{2,0,1:T(1,128)} %param.31) | copy-start | bytes 55300
  19.1 18.2 %copy-start.65 = (bf16[64,1,12,64]{0,3,2,1:T(8,128)(2,1)S(1)}, bf16[64,1,12,64]{0,3,2,1:T(8,128)(2,1)}, u32[]{:S(2)}) copy-start(bf16[64,1,12,64]{0,3,2,1:T(8,128)(2,1)} %copy.275) | copy-start | bytes 294916 | tf_op jit(solution)/shard_map/cond
  45.1 21.6 %copy-start.49 = (bf16[64,768]{1,0:T(8,128)(2,1)}, bf16[64,768]{1,0:T(8,128)(2,1)S(1)}, u32[]{:S(2)}) copy-start(bf16[64,768]{1,0:T(8,128)(2,1)S(1)} %get-tuple-element.675) | copy-start | bytes 294916
  45.1 21.3 %copy-start.39 = (bf16[2,1,64,768]{3,2,1,0:T(8,128)(2,1)S(1)}, bf16[2,1,64,768]{3,2,1,0:T(8,128)(2,1)}, u32[]{:S(2)}) copy-start(bf16[2,1,64,768]{3,2,1,0:T(8,128)(2,1)} %param.22) | copy-start | bytes 589828
  45.1 21.2 %collective-permute-start = (bf16[64,768]{1,0:T(8,128)(2,1)S(1)}, bf16[64,768]{1,0:T(8,128)(2,1)S(1)}, u32[]{:S(2)}, u32[]{:S(2)}) collective-permute-start(bf16[64,768]{1,0:T(8,128)(2,1)S(1)} %get-tuple-element.675), channel_id=1, source_target_pairs={{0,16},{1,17},{2,18},{3,19},{4,20},{5,21},{6,22},{7,23},{8,24},{9,... | collective-permute-start | bytes 294920 | tf_op jit(solution)/shard_map/ppermute | solution.py:17
  47.4 25.4 %copy-start.90 = (f32[768]{0:T(1024)}, f32[768]{0:T(1024)S(1)}, u32[]{:S(2)}) copy-start(f32[768]{0:T(1024)S(1)} %get-tuple-element.490) | copy-start | bytes 9220
  47.4 26.2 %copy-start.69 = (f32[768]{0:T(1024)}, f32[768]{0:T(1024)S(1)}, u32[]{:S(2)}) copy-start(f32[768]{0:T(1024)S(1)} %get-tuple-element.489) | copy-start | bytes 9220
  47.4 82.9 %copy-start.60 = (f32[768]{0:T(1024)}, f32[768]{0:T(1024)S(1)}, u32[]{:S(2)}) copy-start(f32[768]{0:T(1024)S(1)} %get-tuple-element.493) | copy-start | bytes 9220
  48.3 24.6 %copy-start.82 = (f32[768]{0:T(1024)}, f32[768]{0:T(1024)S(1)}, u32[]{:S(2)}) copy-start(f32[768]{0:T(1024)S(1)} %get-tuple-element.497) | copy-start | bytes 9220
  48.3 25.3 %copy-start.57 = (f32[768]{0:T(1024)}, f32[768]{0:T(1024)S(1)}, u32[]{:S(2)}) copy-start(f32[768]{0:T(1024)S(1)} %get-tuple-element.498) | copy-start | bytes 9220
  48.3 25.3 %copy-start.93 = (f32[768]{0:T(1024)}, f32[768]{0:T(1024)S(1)}, u32[]{:S(2)}) copy-start(f32[768]{0:T(1024)S(1)} %get-tuple-element.495) | copy-start | bytes 9220
  81.1 20.3 %copy-start.103 = (pred[64,64]{1,0:T(8,128)(4,1)S(1)}, pred[64,64]{1,0:T(8,128)(4,1)}, u32[]{:S(2)}) copy-start(pred[64,64]{1,0:T(8,128)(4,1)} %get-tuple-element.594) | copy-start | bytes 12292
  81.1 21.6 %copy-start.46 = (bf16[2,1,64,768]{3,2,1,0:T(8,128)(2,1)S(1)}, bf16[2,1,64,768]{3,2,1,0:T(8,128)(2,1)}, u32[]{:S(2)}) copy-start(bf16[2,1,64,768]{3,2,1,0:T(8,128)(2,1)} %param.23) | copy-start | bytes 589828
  81.1 21.7 %copy-start.56 = (f32[1,4,768]{2,1,0:T(4,128)S(1)}, f32[1,4,768]{2,1,0:T(4,128)}, u32[]{:S(2)}) copy-start(f32[1,4,768]{2,1,0:T(4,128)} %param.30) | copy-start | bytes 36868
  81.1 47.8 %collective-permute-start.1 = (bf16[64,768]{1,0:T(8,128)(2,1)}, bf16[64,768]{1,0:T(8,128)(2,1)}, u32[]{:S(2)}, u32[]{:S(2)}) collective-permute-start(bf16[64,768]{1,0:T(8,128)(2,1)} %fusion.336), channel_id=1, source_target_pairs={{0,16},{1,17},{2,18},{3,19},{4,20},{5,21},{6,22},{7,23},{8,24},{9,... | collective-permute-start | bytes 294920 | tf_op jit(solution)/shard_map/ppermute | solution.py:17
  127.6 68.7 %collective-permute-start.2 = (bf16[64,768]{1,0:T(8,128)(2,1)}, bf16[64,768]{1,0:T(8,128)(2,1)}, u32[]{:S(2)}, u32[]{:S(2)}) collective-permute-start(bf16[64,768]{1,0:T(8,128)(2,1)} %convert_element_type.355), channel_id=1, source_target_pairs={{16,0},{17,1},{18,2},{19,3},{20,4},{21,5},{22,6},{23,7},{24,8},{25... | collective-permute-start | bytes 294920 | tf_op jit(solution)/shard_map/ppermute | solution.py:17
  140.6 61.7 %slice-start = ((s8[4718592]{0:T(1024)(128)(4,1)}), s8[524288]{0:T(1024)(128)(4,1)S(1)}, s32[]{:S(2)}) async-start(s8[4718592]{0:T(1024)(128)(4,1)} %bitcast.349), calls=%async_computation.9 | async-start | bytes 1048576
  141.6 54.7 %copy-start.47 = (bf16[2,1,64,768]{3,2,1,0:T(8,128)(2,1)S(1)}, bf16[2,1,64,768]{3,2,1,0:T(8,128)(2,1)}, u32[]{:S(2)}) copy-start(bf16[2,1,64,768]{3,2,1,0:T(8,128)(2,1)} %param.23) | copy-start | bytes 589828
  141.6 54.7 %copy-start.94 = (f32[768]{0:T(1024)S(1)}, f32[768]{0:T(1024)}, u32[]{:S(2)}) copy-start(f32[768]{0:T(1024)} %copy-done.93) | copy-start | bytes 9220
  143.6 61.0 %copy-start.104 = (f32[64]{0:T(128)}, f32[64]{0:T(128)S(1)}, u32[]{:S(2)}) copy-start(f32[64]{0:T(128)S(1)} %broadcast_multiply_fusion.20) | copy-start | bytes 772
  143.8 60.8 %copy-start.118 = (f32[64]{0:T(128)}, f32[64]{0:T(128)S(1)}, u32[]{:S(2)}) copy-start(f32[64]{0:T(128)S(1)} %add_rsqrt_fusion.8) | copy-start | bytes 772
  143.8 58.6 %slice-start.1 = ((s8[4718592]{0:T(1024)(128)(4,1)}), s8[4194304]{0:T(1024)(128)(4,1)S(1)}, s32[]{:S(2)}) async-start(s8[4718592]{0:T(1024)(128)(4,1)} %bitcast.349), calls=%async_computation.10 | async-start | bytes 8388608
  147.3 57.2 %copy-start.14 = (f32[64,3072]{1,0:T(8,128)}, f32[64,3072]{1,0:T(8,128)S(1)}, u32[]{:S(2)}) copy-start(f32[64,3072]{1,0:T(8,128)S(1)} %convolution_add_fusion.22) | copy-start | bytes 2359300
  147.3 55.0 %copy-start.58 = (f32[768]{0:T(1024)S(1)}, f32[768]{0:T(1024)}, u32[]{:S(2)}) copy-start(f32[768]{0:T(1024)} %copy-done.57) | copy-start | bytes 9220
  216.4 11.9 %slice-start.9 = ((s8[4718592]{0:T(1024)(128)(4,1)}), s8[4194304]{0:T(1024)(128)(4,1)S(1)}, s32[]{:S(2)}) async-start(s8[4718592]{0:T(1024)(128)(4,1)} %bitcast.366), calls=%async_computation.18 | async-start | bytes 8388608
  240.7 67.5 %collective-permute-start.3 = (bf16[64,768]{1,0:T(8,128)(2,1)S(1)}, bf16[64,768]{1,0:T(8,128)(2,1)S(1)}, u32[]{:S(2)}, u32[]{:S(2)}) collective-permute-start(bf16[64,768]{1,0:T(8,128)(2,1)S(1)} %convert_element_type.377), channel_id=1, source_target_pairs={{16,0},{17,1},{18,2},{19,3},{20,4},{21,5},{22,6},{23,7},{24,8},{25... | collective-permute-start | bytes 294920 | tf_op jit(solution)/shard_map/ppermute | solution.py:17
  272.1 11.4 copy-start.80
  272.1 12.0 %copy-start.87 = (f32[3072]{0:T(1024)S(1)}, f32[3072]{0:T(1024)}, u32[]{:S(2)}) copy-start(f32[3072]{0:T(1024)} %get-tuple-element.621) | copy-start | bytes 36868
  272.1 13.3 %copy-start.84 = (s32[4096]{0:T(1024)S(1)}, s32[4096]{0:T(1024)}, u32[]{:S(2)}) copy-start(s32[4096]{0:T(1024)} %reshape.690) | copy-start | bytes 49156
  283.5 24.8 %copy-start.48 = (bf16[2,1,64,768]{3,2,1,0:T(8,128)(2,1)S(1)}, bf16[2,1,64,768]{3,2,1,0:T(8,128)(2,1)}, u32[]{:S(2)}) copy-start(bf16[2,1,64,768]{3,2,1,0:T(8,128)(2,1)} %param.23) | copy-start | bytes 589828
  283.5 24.8 %copy-start.29 = (s32[64,64]{1,0:T(8,128)S(1)}, s32[64,64]{1,0:T(8,128)}, u32[]{:S(2)}) copy-start(s32[64,64]{1,0:T(8,128)} %get-tuple-element.601) | copy-start | bytes 49156
  283.5 24.8 %copy-start.52 = (f32[1,6,768]{2,1,0:T(8,128)S(1)}, f32[1,6,768]{2,1,0:T(8,128)}, u32[]{:S(2)}) copy-start(f32[1,6,768]{2,1,0:T(8,128)} %copy-done.51) | copy-start | bytes 55300
  283.5 24.8 %copy-start.72 = (pred[64,64]{0,1:T(8,128)(4,1)S(1)}, pred[64,64]{0,1:T(8,128)(4,1)}, u32[]{:S(2)}) copy-start(pred[64,64]{0,1:T(8,128)(4,1)} %copy-done.71) | copy-start | bytes 12292
  308.3 28.7 %copy-start.31 = (s32[64,64]{1,0:T(8,128)}, s32[64,64]{1,0:T(8,128)S(1)}, u32[]{:S(2)}) copy-start(s32[64,64]{1,0:T(8,128)S(1)} %get-tuple-element.269) | copy-start | bytes 49156 | tf_op jit(solution)/shard_map/cond
  308.3 43.8 %copy-start.16 = (f32[64,768]{1,0:T(8,128)}, f32[64,768]{1,0:T(8,128)S(1)}, u32[]{:S(2)}) copy-start(f32[64,768]{1,0:T(8,128)S(1)} %get-tuple-element.260) | copy-start | bytes 589828 | tf_op jit(solution)/shard_map/cond
  310.9 31.3 %copy-start.96 = (f32[768]{0:T(1024)}, f32[768]{0:T(1024)S(1)}, u32[]{:S(2)}) copy-start(f32[768]{0:T(1024)S(1)} %get-tuple-element.470) | copy-start | bytes 9220 | tf_op jit(solution)/shard_map/cond
  317.3 21.2 %copy-start.20 = (bf16[64,1,12,64]{3,2,1,0:T(8,128)(2,1)}, bf16[64,1,12,64]{3,2,1,0:T(8,128)(2,1)S(1)}, u32[]{:S(2)}) copy-start(bf16[64,1,12,64]{3,2,1,0:T(8,128)(2,1)S(1)} %get-tuple-element.569) | copy-start | bytes 294916 | tf_op jit(solution)/shard_map/cond
  317.3 21.2 %copy-start.21 = (bf16[64,1,12,64]{3,2,1,0:T(8,128)(2,1)}, bf16[64,1,12,64]{3,2,1,0:T(8,128)(2,1)S(1)}, u32[]{:S(2)}) copy-start(bf16[64,1,12,64]{3,2,1,0:T(8,128)(2,1)S(1)} %get-tuple-element.571) | copy-start | bytes 294916 | tf_op jit(solution)/shard_map/cond
  342.0 10.1 copy-start.116
  342.2 9.9 copy-start.124
  363.3 9.9 slice-start.6
  363.3 9.9 slice-start.7
  416.6 241.0 %reduce-scatter.7.cloned.1.call-start = ((), (), s32[]{:S(2)}) async-start(), calls=%async_computation.5 | async-start | bytes 2506752 | tf_op jit(solution)/shard_map/reduce_scatter | solution.py:282
  417.3 396.8 %reduce-scatter.5.cloned.1.call-start = ((), (), s32[]{:S(2)}) async-start(), calls=%async_computation.4 | async-start | bytes 7520256 | tf_op jit(solution)/shard_map/reduce_scatter | solution.py:281
  418.1 572.2 %reduce-scatter.9.cloned.1.call-start = ((), (), s32[]{:S(2)}) async-start(), calls=%async_computation.6 | async-start | bytes 10027008 | tf_op jit(solution)/shard_map/reduce_scatter | solution.py:283
  418.6 747.9 %reduce-scatter.11.cloned.1.call-start = ((), (), s32[]{:S(2)}) async-start(), calls=%async_computation.7 | async-start | bytes 10027008 | tf_op jit(solution)/shard_map/reduce_scatter | solution.py:284
  (89 other events, 447.2 us)
Sparse Core Ops, SparseCore 0:
  416.7 107.7 all-reduce.2
  530.0 127.5 reduce-scatter.6
  664.3 149.7 reduce-scatter.4
  821.2 169.0 reduce-scatter.8
  996.3 170.1 reduce-scatter.10
where the time goes:
time: 1190 us; the launch traced here: 1180 us
  waiting for transfers between devices  793 us (67%)
  local copies, waits for them, and re-layouts  128 us (11%)
  other arithmetic  115 us (10%)
  matrix products  111 us (9%)
  between operations  15.2 us (1%)
    reduce_scatter x1, waiting for transfers between devices, per_device(): lax.psum_scatter(totals[3], 'batch', scatter_dimension=0, tiled=True)  176 us
    reduce_scatter x1, waiting for transfers between devices, per_device(): lax.psum_scatter(totals[2], 'batch', scatter_dimension=0, tiled=True)  176 us
    reduce_scatter x1, waiting for transfers between devices, per_device(): lax.psum_scatter(totals[0], 'batch', scatter_dimension=0, tiled=True)  157 us
    reduce_scatter x1, waiting for transfers between devices, per_device(): lax.psum_scatter(totals[1], 'batch', scatter_dimension=0, tiled=True)  133 us
    psum x1, waiting for transfers between devices, per_device(): lax.psum((totals[4], totals[5], totals[6], totals[7]), 'batch')  99.9 us
    gather x8, local copies, waits for them, and re-layouts, forward(): pos_bias = jnp.take(pos_table, rel_index, axis=1)  68.8 us
    ppermute x4, waiting for transfers between devices, passed_along(): lax.ppermute(value, axis, [(source, source + steps) for source in range(l...  49 us
    scatter-add x2, other arithmetic, backward(): jax.ops.segment_sum(head_vals, flat_index, num_segments=rel_count)  45.6 us
  transfers between devices with their start and end apart: 9, of which 6 were waited for; matrix products, arithmetic and copies ran while one was open for 12% of the time, Pallas kernels for 0%

commit v1 on v0

v1 whole, which is shorter than its diff:
```python
import functools

import jax
import jax.numpy as jnp
from jax import lax
from jax.experimental import pallas as pl
from jax.experimental.pallas import tpu as pltpu
from jax.sharding import PartitionSpec as P

MESH = pl.DeviceIdType.MESH
F32 = jnp.float32
BF16 = jnp.bfloat16
REACH = 13
SPAN = 2 * REACH + 1
NORM_EPS = 1e-06
ROOT_HALF = 0.7071067811865476
INV_ROOT_TWO_PI = 0.3989422804014327
COLS = 256
GRID_ROWS = 8
GRID_COLS = 16
PITCH = 2 * GRID_COLS
WIDE = 2 * GRID_ROWS * PITCH
HALF = WIDE // 2


def nn(left, right):
    return lax.dot_general(left, right, (((1,), (0,)), ((), ())), preferred_element_type=F32)


def nt(left, right):
    return lax.dot_general(left, right, (((1,), (1,)), ((), ())), preferred_element_type=F32)


def tn(left, right):
    return lax.dot_general(left, right, (((0,), (0,)), ((), ())), preferred_element_type=F32)


def iota(shape, dim):
    return lax.broadcasted_iota(jnp.int32, shape, dim)


def two_parts(value):
    high = value.astype(BF16)
    return high, (value - high.astype(F32)).astype(BF16)


def norm_parts(values_in):
    row_mean = jnp.mean(values_in, axis=-1, keepdims=True)
    centered = values_in - row_mean
    inv_scale = lax.rsqrt(jnp.mean(centered * centered, axis=-1, keepdims=True) + NORM_EPS)
    return centered * inv_scale, inv_scale


def norm_back(upstream, normal_in, inv_scale):
    return inv_scale * (
        upstream
        - jnp.mean(upstream, axis=-1, keepdims=True)
        - normal_in * jnp.mean(upstream * normal_in, axis=-1, keepdims=True)
    )


def col_sum(value):
    return jnp.sum(value, axis=0, keepdims=True)


def chunk_loop(count, body):
    def step(index, carry):
        body(index)
        return carry

    lax.fori_loop(0, count, step, 0)


def cols_of(index, size=COLS):
    return pl.ds(pl.multiple_of(index * size, size), size)


def geometry(seg, wid, same, pick_q, pick_k, pick_kt, pick_qt):
    micro, slots = seg.shape
    tokens = micro * slots
    images = wid.shape[1]
    seg_f = seg[...].astype(F32)
    seg_row = jnp.concatenate(
        [seg_f[m : m + 1, :] + float(m * images) for m in range(micro)], axis=1
    )
    sub = iota((tokens, tokens), 0)
    lane = iota((tokens, tokens), 1)
    seg_col = jnp.sum(jnp.where(sub == lane, seg_row, 0.0), axis=1, keepdims=True)
    same[...] = (seg_col == seg_row).astype(F32)
    before_row = jnp.sum((seg_col < seg_row).astype(F32), axis=0, keepdims=True)
    before_col = jnp.sum((seg_row < seg_col).astype(F32), axis=1, keepdims=True)
    place_row = iota((1, tokens), 1).astype(F32) - before_row
    place_col = iota((tokens, 1), 0).astype(F32) - before_col
    width_row = jnp.zeros((1, tokens), F32)
    width_col = jnp.zeros((tokens, 1), F32)
    for m in range(micro):
        for image in range(images):
            width = wid[m, image].astype(F32)
            number = float(m * images + image)
            width_row = width_row + jnp.where(seg_row == number, width, 0.0)
            width_col = width_col + jnp.where(seg_col == number, width, 0.0)

    def grid(place, width):
        row = jnp.zeros_like(place)
        for k in range(1, GRID_ROWS):
            row = row + (place >= float(k) * width).astype(F32)
        return row, place - row * width

    row_r, col_r = grid(place_row, width_row)
    row_c, col_c = grid(place_col, width_col)
    cells = GRID_ROWS * GRID_COLS
    pick_q[...] = (iota((tokens, cells), 1).astype(F32) == row_c * GRID_COLS + col_c).astype(
        F32
    ).astype(BF16)
    pick_qt[...] = (
        iota((cells, tokens), 0).astype(F32) == row_r * GRID_COLS + (GRID_COLS - 1.0) - col_r
    ).astype(F32).astype(BF16)
    pick_k[...] = (iota((tokens, HALF), 1).astype(F32) == row_c * PITCH + col_c).astype(
        F32
    ).astype(BF16)
    pick_kt[...] = (iota((HALF, tokens), 0).astype(F32) == row_r * PITCH + col_r).astype(
        F32
    ).astype(BF16)


def spread_table(table, padded, spread, wide_table):
    heads, rels = table.shape
    padded[...] = jnp.zeros_like(padded)
    padded[0:heads, 0:rels] = table[...]
    shape = spread.shape
    where = iota((1, WIDE), 1)
    signed = jnp.where(where < HALF, where, where - WIDE)
    row_step = (signed + GRID_COLS + WIDE) // PITCH - WIDE // PITCH
    col_step = signed - row_step * PITCH
    entry = (REACH - row_step) * SPAN + jnp.clip(-col_step, -REACH, REACH) + REACH
    spread[...] = (iota(shape, 0) == entry).astype(F32).astype(BF16)
    high, low = two_parts(padded[...])
    vector = nn(high, spread[...]) + nn(low, spread[...])
    cells = GRID_ROWS * GRID_COLS
    for head in range(heads):
        line = jnp.broadcast_to(vector[head : head + 1, :], (GRID_COLS, WIDE))
        line = pltpu.roll(line, 0, 1, stride=1, stride_axis=0)
        for low_row in range(4):
            turned = line if low_row == 0 else pltpu.roll(line, low_row * PITCH, 1)
            for high_row in range(GRID_ROWS // 4):
                if high_row == 0:
                    part = turned[:, 0:HALF]
                else:
                    part = jnp.concatenate(
                        [turned[:, WIDE - 4 * PITCH : WIDE], turned[:, 0 : HALF - 4 * PITCH]], axis=1
                    )
                top = (high_row * 4 + low_row) * GRID_COLS
                part_high, part_low = two_parts(part)
                wide_table[top : top + GRID_COLS, head * HALF : (head + 1) * HALF] = part_high
                wide_table[
                    cells + top : cells + top + GRID_COLS, head * HALF : (head + 1) * HALF
                ] = part_low


def fold_table(head_grad):
    total = None
    for low_row in range(4):
        near = head_grad[low_row * GRID_COLS : (low_row + 1) * GRID_COLS, :]
        far = head_grad[(low_row + 4) * GRID_COLS : (low_row + 5) * GRID_COLS, :]
        step = 4 * PITCH
        laid = jnp.concatenate(
            [
                near[:, 0:step] + far[:, step : 2 * step],
                near[:, step : 2 * step],
                jnp.zeros((GRID_COLS, step), F32),
                far[:, 0:step],
            ],
            axis=1,
        )
        if low_row > 0:
            laid = pltpu.roll(laid, WIDE - low_row * PITCH, 1)
        total = laid if total is None else total + laid
    total = pltpu.roll(total, WIDE - (GRID_COLS - 1), 1, stride=1, stride_axis=0)
    return col_sum(total)


def block_kernel(
    inputs,
    cotangent,
    seg,
    wid,
    wqkv_in,
    wout_in,
    wfc1_in,
    wfc2_in,
    gains,
    biases,
    fc1_bias,
    table,
    activation,
    grad_in,
    at_small,
    at_active,
    b_all,
    small,
    wqkv,
    wout,
    wfc1,
    wfc2,
    arrived,
    leaving,
    stream,
    hat_one,
    hat_two,
    att_out,
    branch,
    d_middle,
    d_wide,
    normed,
    qkv,
    probs,
    bias,
    mixed,
    d_mixed,
    second,
    active,
    slope,
    same,
    pick_q,
    pick_k,
    pick_kt,
    pick_qt,
    padded,
    spread,
    wide_table,
    folded,
    scale_one,
    scale_two,
    weight_sem,
    send_sem,
    recv_sem,
):
    section = lax.axis_index("section")
    place = lax.axis_index("batch")
    other = (1 - section, place)
    width = inputs.shape[1]
    tokens = inputs.shape[0]
    ff = active.shape[1]
    heads = table.shape[0]
    pair = 2 * (width // heads)
    pairs = heads // 2
    parts = ff // width
    per_part = width // COLS

    loads = [
        pltpu.make_async_copy(source.at[0], target, weight_sem.at[index])
        for index, (source, target) in enumerate(
            [(wqkv_in, wqkv), (wout_in, wout), (wfc1_in, wfc1), (wfc2_in, wfc2)]
        )
    ]
    for load in loads:
        load.start()

    barrier = pltpu.get_barrier_semaphore()
    pl.semaphore_signal(barrier, inc=1, device_id=other, device_id_type=MESH)

    geometry(seg, wid, same, pick_q, pick_k, pick_kt, pick_qt)
    spread_table(table, padded, spread, wide_table)
    cells = GRID_ROWS * GRID_COLS

    def bias_of(head):
        where = cols_of(head, HALF)
        high = nn(pick_q[...], wide_table[0:cells, where]).astype(BF16)
        low = nn(pick_q[...], wide_table[cells : 2 * cells, where]).astype(BF16)
        bias[cols_of(head, tokens), :] = nn(high, pick_kt[...]) + nn(low, pick_kt[...])

    chunk_loop(heads, bias_of)

    pl.semaphore_wait(barrier, 1)

    def relay(source):
        return pltpu.make_async_remote_copy(
            src_ref=source,
            dst_ref=arrived,
            send_sem=send_sem,
            recv_sem=recv_sem,
            device_id=other,
            device_id_type=MESH,
        )

    @pl.when(section == 0)
    def _():
        stream[...] = inputs[...].astype(F32)

    @pl.when(section == 1)
    def _():
        relay(activation).wait_recv()
        stream[...] = arrived[...].astype(F32)

    hat, inv_scale = norm_parts(stream[...])
    hat_one[...] = hat
    scale_one[...] = inv_scale
    normed[...] = (hat * gains[0, 0:1, :] + biases[0, 0:1, :]).astype(BF16)
    loads[0].wait()
    for third in range(3):

        def project(index):
            out = nn(normed[...], wqkv[:, cols_of(third * per_part + index)])
            if third != 1:
                row = 1 if third == 0 else 2
                out = out + biases[0, row : row + 1, cols_of(index)]
            qkv[third, :, cols_of(index)] = out.astype(BF16)

        chunk_loop(per_part, project)

    lane = iota((1, pair), 1)
    low_lanes = (lane < pair // 2).astype(F32).astype(BF16)
    high_lanes = (lane >= pair // 2).astype(F32).astype(BF16)

    def stacked(value):
        return jnp.concatenate([value * low_lanes, value * high_lanes], axis=0)

    def side_by_side(value):
        return jnp.concatenate([value[0:tokens, :], value[tokens : 2 * tokens, :]], axis=1)

    for index in range(pairs):
        at = slice(index * pair, (index + 1) * pair)
        rows = slice(index * 2 * tokens, (index + 1) * 2 * tokens)
        raw = nt(stacked(qkv[0, :, at]), qkv[1, :, at])
        mask = jnp.concatenate([same[...], same[...]], axis=0) > 0.5
        scores = jnp.where(mask, raw * 0.125 + bias[rows, :], -1e30)
        exped = jnp.exp(scores - jnp.max(scores, axis=-1, keepdims=True))
        prob = exped / jnp.sum(exped, axis=-1, keepdims=True)
        probs[rows, :] = prob
        mixed[:, at] = nn(side_by_side(prob.astype(BF16)), stacked(qkv[2, :, at])).astype(BF16)

    loads[1].wait()

    def attend_out(index):
        at = cols_of(index)
        out = nn(mixed[...], wout[:, at]) + biases[0, 3:4, at]
        att_out[:, at] = out
        stream[:, at] = stream[:, at] + gains[0, 1:2, at] * out

    chunk_loop(per_part, attend_out)
    hat, inv_scale = norm_parts(stream[...])
    hat_two[...] = hat
    scale_two[...] = inv_scale
    second[...] = (hat * gains[0, 2:3, :] + biases[0, 4:5, :]).astype(BF16)
    loads[2].wait()

    def feed(index):
        at = cols_of(index)
        hidden = nn(second[...], wfc1[:, at]) + fc1_bias[0:1, at]
        cumul = 0.5 * (1.0 + lax.erf(hidden * ROOT_HALF))
        density = jnp.exp(-0.5 * hidden * hidden) * INV_ROOT_TWO_PI
        active[:, at] = (hidden * cumul).astype(BF16)
        slope[:, at] = cumul + hidden * density

    chunk_loop(ff // COLS, feed)
    loads[3].wait()

    def feed_out(index):
        at = cols_of(index)
        out = nn(active[...], wfc2[:, at]) + biases[0, 5:6, at]
        branch[:, at] = out
        activation[:, at] = (stream[:, at] + gains[0, 3:4, at] * out).astype(BF16)

    chunk_loop(per_part, feed_out)

    def turn():
        def turn_small(index):
            at = cols_of(index, 128)
            for number, source in enumerate((second, normed, mixed)):
                at_small[number, at, :] = source[:, at].T

        def turn_active(index):
            at = cols_of(index, 128)
            at_active[at, :] = active[:, at].T

        chunk_loop(width // 128, turn_small)
        chunk_loop(ff // 128, turn_active)

    @pl.when(section == 0)
    def _():
        relay(activation).start()
        turn()
        relay(activation).wait_send()
        relay(activation).wait_recv()
        stream[...] = arrived[...].astype(F32)

    @pl.when(section == 1)
    def _():
        stream[...] = cotangent[...].astype(F32)

    small[...] = jnp.zeros_like(small)
    upstream = stream[...]
    small[3:4, :] = col_sum(upstream * branch[...])
    d_branch = (gains[0, 3:4, :] * upstream).astype(BF16)
    b_all[parts + 4] = d_branch
    small[9:10, :] = col_sum(d_branch.astype(F32))

    def feed_back(index):
        at = cols_of(index)
        out = nt(b_all[parts + 4], wfc2[at, :])
        d_hidden = (out * slope[:, at]).astype(BF16)
        part = index // per_part
        inner = cols_of(index % per_part)
        b_all[part, :, inner] = d_hidden
        small[pl.ds(10 + part, 1), inner] = col_sum(d_hidden.astype(F32))

    chunk_loop(ff // COLS, feed_back)

    def second_back(index):
        at = cols_of(index)
        out = nt(b_all[0], wfc1[at, 0:width])
        for part in range(1, parts):
            out = out + nt(b_all[part], wfc1[at, part * width : (part + 1) * width])
        d_wide[:, at] = out

    chunk_loop(per_part, second_back)
    d_second = d_wide[...]
    small[2:3, :] = col_sum(d_second * hat_two[...])
    small[8:9, :] = col_sum(d_second)
    d_mid = stream[...] + norm_back(d_second * gains[0, 2:3, :], hat_two[...], scale_two[...])
    d_middle[...] = d_mid
    small[1:2, :] = col_sum(d_mid * att_out[...])
    d_att = (gains[0, 1:2, :] * d_mid).astype(BF16)
    b_all[parts + 3] = d_att
    small[7:8, :] = col_sum(d_att.astype(F32))

    def out_back(index):
        at = cols_of(index)
        d_mixed[:, at] = nt(b_all[parts + 3], wout[at, :]).astype(BF16)

    chunk_loop(per_part, out_back)

    folded[...] = jnp.zeros_like(folded)
    for index in range(pairs):
        at = slice(index * pair, (index + 1) * pair)
        rows = slice(index * 2 * tokens, (index + 1) * 2 * tokens)
        prob = probs[rows, :]
        d_mix = stacked(d_mixed[:, at])
        d_prob = nt(d_mix, qkv[2, :, at])
        b_all[parts + 2, :, at] = tn(prob.astype(BF16), d_mix).astype(BF16)
        d_scores = prob * (d_prob - jnp.sum(prob * d_prob, axis=-1, keepdims=True))
        d_raw = (0.125 * d_scores).astype(BF16)
        b_all[parts, :, at] = nn(side_by_side(d_raw), stacked(qkv[1, :, at])).astype(BF16)
        b_all[parts + 1, :, at] = tn(d_raw, stacked(qkv[0, :, at])).astype(BF16)
        high, low = two_parts(d_scores)
        high = nn(high, pick_k[...]).astype(BF16)
        low = nn(low, pick_k[...]).astype(BF16)
        for side in range(2):
            own = slice(side * tokens, (side + 1) * tokens)
            head_grad = nn(pick_qt[...], high[own, :]) + nn(pick_qt[...], low[own, :])
            folded[2 * index + side : 2 * index + side + 1, :] = fold_table(head_grad)

    small[5:6, :] = col_sum(b_all[parts].astype(F32))
    small[6:7, :] = col_sum(b_all[parts + 2].astype(F32))

    def normed_back(index):
        at = cols_of(index)
        out = nt(b_all[parts], wqkv[at, 0:width])
        for third in range(1, 3):
            out = out + nt(b_all[parts + third], wqkv[at, third * width : (third + 1) * width])
        d_wide[:, at] = out

    chunk_loop(per_part, normed_back)
    d_normed = d_wide[...]
    small[0:1, :] = col_sum(d_normed * hat_one[...])
    small[4:5, :] = col_sum(d_normed)
    d_in = d_middle[...] + norm_back(d_normed * gains[0, 0:1, :], hat_one[...], scale_one[...])
    grad_in[...] = d_in
    leaving[...] = d_in.astype(BF16)

    @pl.when(section == 1)
    def _():
        relay(leaving).start()
        turn()

    high, low = two_parts(folded[...])
    small[16:32, :] = nt(high, spread[...]) + nt(low, spread[...])

    @pl.when(section == 1)
    def _():
        relay(leaving).wait_send()


def run_block(inputs, cotangent, seg, wid, weights):
    w_qkv, w_out, w_fc1, w_fc2, gains, biases, fc1_bias, table = weights
    tokens, width = inputs.shape
    ff = w_fc1.shape[2]
    heads, rels = table.shape[1:]
    parts = ff // width
    cells = GRID_ROWS * GRID_COLS
    whole = pl.BlockSpec(memory_space=pltpu.VMEM)
    vm = pltpu.VMEM
    padded_rels = -(-rels // 256) * 256
    return pl.pallas_call(
        block_kernel,
        out_shape=(
            jax.ShapeDtypeStruct((tokens, width), BF16),
            jax.ShapeDtypeStruct((tokens, width), F32),
            jax.ShapeDtypeStruct((3, width, tokens), BF16),
            jax.ShapeDtypeStruct((ff, tokens), BF16),
            jax.ShapeDtypeStruct((parts + 5, tokens, width), BF16),
            jax.ShapeDtypeStruct((32, width), F32),
        ),
        in_specs=[whole, whole, whole, pl.BlockSpec(memory_space=pltpu.SMEM)]
        + [pl.BlockSpec(memory_space=pl.ANY)] * 4
        + [whole] * 4,
        out_specs=(whole,) * 6,
        scratch_shapes=[
            vm(w_qkv.shape[1:], BF16),
            vm(w_out.shape[1:], BF16),
            vm(w_fc1.shape[1:], BF16),
            vm(w_fc2.shape[1:], BF16),
            vm((tokens, width), BF16),
            vm((tokens, width), BF16),
        ]
        + [vm((tokens, width), F32)] * 7
        + [
            vm((tokens, width), BF16),
            vm((3, tokens, width), BF16),
            vm((heads * tokens, tokens), F32),
            vm((heads * tokens, tokens), F32),
            vm((tokens, width), BF16),
            vm((tokens, width), BF16),
            vm((tokens, width), BF16),
            vm((tokens, ff), BF16),
            vm((tokens, ff), F32),
            vm((tokens, tokens), F32),
            vm((tokens, cells), BF16),
            vm((tokens, HALF), BF16),
            vm((HALF, tokens), BF16),
            vm((cells, tokens), BF16),
            vm((16, padded_rels), F32),
            vm((padded_rels, WIDE), BF16),
            vm((2 * cells, heads * HALF), BF16),
            vm((16, WIDE), F32),
            vm((tokens, 1), F32),
            vm((tokens, 1), F32),
            pltpu.SemaphoreType.DMA((4,)),
            pltpu.SemaphoreType.DMA,
            pltpu.SemaphoreType.DMA,
        ],
        compiler_params=pltpu.CompilerParams(
            collective_id=0, has_side_effects=True, vmem_limit_bytes=56 * 2**20
        ),
        name="block",
    )(inputs, cotangent, seg, wid, w_qkv, w_out, w_fc1, w_fc2, gains, biases, fc1_bias, table[0])


UNIT_LEFT = (0, 0, 0, 0, 1, 1, 1, 2)


def share_kernel(
    at_small,
    at_active,
    b_all,
    small,
    g_qkv,
    g_out,
    g_fc1,
    g_fc2,
    g_gains,
    g_biases,
    g_fc1_bias,
    g_table,
    left,
    right,
    left_four,
    right_four,
    y_send,
    y_recv,
    totals,
    passing,
    inward,
    small_own,
    small_recv,
    own_sem,
    x_send_sem,
    x_recv_sem,
    y_send_sem,
    y_recv_sem,
    four_send_sem,
    four_recv_sem,
    z_send_sem,
    z_recv_sem,
    small_send_sem,
    small_recv_sem,
):
    section = lax.axis_index("section")
    place = lax.axis_index("batch")
    z = place // 4
    y = (place // 2) % 2
    x = place % 2
    x_peer = z * 4 + y * 2 + (1 - x)
    y_peer = z * 4 + (1 - y) * 2 + x
    xy_peer = z * 4 + (1 - y) * 2 + (1 - x)
    at_end = (z == 0) | (z == 3)
    lower = z < 2
    in_peer = jnp.where(lower, place + 4, place - 4)
    out_peer = jnp.where(z == 1, place - 4, place + 4)
    out_peer = jnp.where(at_end, place, out_peer)
    far_z = jnp.where(lower, z + 2, z - 2)
    far_peer = far_z * 4 + y * 2 + x
    pair_peer = jnp.where(z % 2 == 0, place + 4, place - 4)
    units = len(UNIT_LEFT)
    tokens = b_all.shape[1]
    rows = left.shape[3]
    width = right.shape[2]

    def remote(source, target, send, recv, peer):
        return pltpu.make_async_remote_copy(
            src_ref=source,
            dst_ref=target,
            send_sem=send,
            recv_sem=recv,
            device_id=(section, peer),
            device_id_type=MESH,
        )

    barrier = pltpu.get_barrier_semaphore()

    def greet(peer):
        pl.semaphore_signal(barrier, inc=1, device_id=(section, peer), device_id_type=MESH)

    for peer in (x_peer, y_peer, xy_peer, in_peer, far_peer):
        greet(peer)

    @pl.when(jnp.logical_not(at_end))
    def _():
        greet(out_peer)

    own = []
    for number in range(3):
        own.append(
            pltpu.make_async_copy(
                at_small.at[number, :, :, x],
                left.at[number, :, :, :, 0:tokens],
                own_sem.at[number],
            )
        )
    own.append(
        pltpu.make_async_copy(
            b_all.at[0:units], right.at[:, 0:tokens, :], own_sem.at[3]
        )
    )
    own.append(
        pltpu.make_async_copy(at_active.at[:, y, x], left_four.at[:, :, 0:tokens], own_sem.at[4])
    )
    own.append(
        pltpu.make_async_copy(b_all.at[units], right_four.at[0:tokens, :], own_sem.at[5])
    )
    for copy in own:
        copy.start()
    small_own[0] = small[...]

    @pl.when(at_end)
    def _():
        pl.semaphore_wait(barrier, 5)

    @pl.when(jnp.logical_not(at_end))
    def _():
        pl.semaphore_wait(barrier, 6)

    def send_four(slot, peer_y, peer_x, peer):
        lanes = slice(slot * tokens, (slot + 1) * tokens)
        return (
            remote(
                at_active.at[:, peer_y, peer_x],
                left_four.at[:, :, lanes],
                four_send_sem.at[0, slot],
                four_recv_sem.at[0, slot],
                peer,
            ),
            remote(
                b_all.at[units],
                right_four.at[lanes, :],
                four_send_sem.at[1, slot],
                four_recv_sem.at[1, slot],
                peer,
            ),
        )

    four = (
        send_four(1, y, 1 - x, x_peer)
        + send_four(2, 1 - y, x, y_peer)
        + send_four(3, 1 - y, 1 - x, xy_peer)
    )
    x_left = [
        remote(
            at_small.at[number, :, :, 1 - x],
            left.at[number, :, :, :, tokens : 2 * tokens],
            x_send_sem.at[units + number],
            x_recv_sem.at[units + number],
            x_peer,
        )
        for number in range(3)
    ]
    x_right = [
        remote(
            b_all.at[unit],
            right.at[unit, tokens : 2 * tokens, :],
            x_send_sem.at[unit],
            x_recv_sem.at[unit],
            x_peer,
        )
        for unit in range(units)
    ]
    small_peers = (x_peer, y_peer, pair_peer, far_peer)
    small_copy = [
        remote(
            small_own.at[step],
            small_recv.at[step],
            small_send_sem.at[step],
            small_recv_sem.at[step],
            small_peers[step],
        )
        for step in range(4)
    ]
    small_copy[0].start()
    x_left[0].start()
    x_right[0].start()
    for copy in four[2:4]:
        copy.start()
    x_right[1].start()
    for copy in four[4:6]:
        copy.start()
    x_right[2].start()
    x_right[3].start()
    for copy in four[0:2]:
        copy.start()
    x_left[1].start()
    for unit in (4, 5, 6):
        x_right[unit].start()
    x_left[2].start()
    x_right[7].start()

    y_copy = [
        remote(
            y_send.at[unit],
            y_recv.at[unit],
            y_send_sem.at[unit],
            y_recv_sem.at[unit],
            y_peer,
        )
        for unit in range(units)
    ]
    order = [0, 1, 2, 3, 8, 4, 9, 5, 10, 6, 11, 7]
    for copy in own:
        copy.wait()
    waited = set()

    def product(unit, side):
        lhs = left[UNIT_LEFT[unit], :, side].reshape(4 * rows, 2 * tokens)
        return nn(lhs, right[unit])

    def first(unit):
        if unit >= units:
            if not waited & {"four"}:
                waited.add("four")
                for copy in four:
                    copy.wait_recv()
            return
        if UNIT_LEFT[unit] not in waited:
            waited.add(UNIT_LEFT[unit])
            x_left[UNIT_LEFT[unit]].wait_recv()
        x_right[unit].wait_recv()
        y_send[unit] = product(unit, 1 - y).astype(BF16).reshape(4, rows, width)
        y_copy[unit].start()

    def z_copy(unit, dest, peer, final_inside):
        target = inward.at[unit] if final_inside else passing.at[unit, dest]
        slot = 4 if final_inside else dest
        return remote(
            totals.at[unit, dest],
            target,
            z_send_sem.at[unit, dest],
            z_recv_sem.at[unit, slot],
            peer,
        )

    far_end = jnp.where(lower, 3, 0)
    far_mid = jnp.where(lower, 2, 1)
    near_mid = jnp.where(lower, 1, 2)
    near_end = jnp.where(lower, 0, 3)

    def add_passing(unit, dest):
        totals[unit, dest] = (
            totals[unit, dest].astype(F32) + passing[unit, dest].astype(F32)
        ).astype(BF16)

    def second(unit):
        if unit >= units:
            piece = slice((unit - units) * rows, (unit - units + 1) * rows)
            lhs = left_four[:, piece, :].reshape(4 * rows, 4 * tokens)
            out = nn(lhs, right_four[...])
        else:
            out = product(unit, y)
            y_copy[unit].wait_recv()
            out = out + y_recv[unit].reshape(4 * rows, width).astype(F32)
        totals[unit] = out.astype(BF16).reshape(4, rows, width)

        @pl.when(at_end)
        def _():
            z_copy(unit, far_end, in_peer, False).start()
            z_copy(unit, far_mid, in_peer, False).start()
            z_copy(unit, near_mid, in_peer, False).start()

    def third(unit):
        @pl.when(jnp.logical_not(at_end))
        def _():
            z_copy(unit, far_end, in_peer, False).wait_recv()
            add_passing(unit, far_end)
            z_copy(unit, far_end, in_peer, False).start()
            z_copy(unit, far_mid, in_peer, False).wait_recv()
            add_passing(unit, far_mid)
            z_copy(unit, far_mid, in_peer, True).start()

    def fourth(unit):
        @pl.when(jnp.logical_not(at_end))
        def _():
            z_copy(unit, near_end, out_peer, False).wait_recv()
            add_passing(unit, near_end)
            z_copy(unit, near_end, out_peer, True).start()

    def store(unit, value):
        if unit < 4:
            g_fc1[:, unit * width : (unit + 1) * width] = value
        elif unit < 7:
            g_qkv[:, (unit - 4) * width : (unit - 3) * width] = value
        elif unit == 7:
            g_out[...] = value
        else:
            g_fc2[(unit - units) * rows : (unit - units + 1) * rows, :] = value

    def fifth(unit):
        z_copy(unit, z, in_peer, True).wait_recv()
        value = totals[unit, z].astype(F32) + inward[unit].astype(F32)

        @pl.when(at_end)
        def _():
            store(unit, value)

        @pl.when(jnp.logical_not(at_end))
        def _():
            z_copy(unit, z, in_peer, False).wait_recv()
            store(unit, value + passing[unit, z].astype(F32))

    def small_step(step):
        small_copy[step].wait_recv()
        small_own[step + 1] = small_own[step] + small_recv[step]
        if step < 3:
            small_copy[step + 1].start()

    stages = (first, second, third, fourth, fifth)
    for turn in range(len(order) + len(stages) - 1):
        for depth in (0, 1, 2, 3, 4):
            index = turn - depth
            if 0 <= index < len(order):
                stages[depth](order[index])
        if turn < 4:
            small_step(turn)

    g_gains[...] = small_own[4, 0:4, :]
    g_biases[...] = small_own[4, 4:10, :]
    for part in range(4):
        g_fc1_bias[0:1, part * width : (part + 1) * width] = small_own[4, 10 + part : 11 + part, :]
    g_table[...] = small_own[4, 16 : 16 + g_table.shape[0], 0 : g_table.shape[1]]

    for copy in four:
        copy.wait_send()
    for copy in x_left + x_right + y_copy + small_copy:
        copy.wait_send()

    @pl.when(at_end)
    def _():
        for unit in order:
            z_copy(unit, far_end, in_peer, False).wait_send()
            z_copy(unit, far_mid, in_peer, False).wait_send()
            z_copy(unit, near_mid, in_peer, False).wait_send()

    @pl.when(jnp.logical_not(at_end))
    def _():
        for unit in order:
            z_copy(unit, far_end, in_peer, False).wait_send()
            z_copy(unit, far_mid, in_peer, True).wait_send()
            z_copy(unit, near_end, out_peer, True).wait_send()


def run_shares(at_small, at_active, b_all, small, heads, rels):
    width, tokens = at_small.shape[1:]
    ff = at_active.shape[0]
    rows = width // 16
    units = len(UNIT_LEFT)
    all_units = units + ff // width
    at_small = at_small.reshape(3, 4, 2, 2, rows, tokens)
    at_active = at_active.reshape(4, 2, 2, ff // 16, tokens)
    whole = pl.BlockSpec(memory_space=pltpu.VMEM)
    anywhere = pl.BlockSpec(memory_space=pl.ANY)
    vm = pltpu.VMEM
    dma = pltpu.SemaphoreType.DMA
    return pl.pallas_call(
        share_kernel,
        out_shape=(
            jax.ShapeDtypeStruct((rows, 3 * width), F32),
            jax.ShapeDtypeStruct((rows, width), F32),
            jax.ShapeDtypeStruct((rows, ff), F32),
            jax.ShapeDtypeStruct((ff // 16, width), F32),
            jax.ShapeDtypeStruct((4, width), F32),
            jax.ShapeDtypeStruct((6, width), F32),
            jax.ShapeDtypeStruct((1, ff), F32),
            jax.ShapeDtypeStruct((heads, rels), F32),
        ),
        in_specs=[anywhere, anywhere, anywhere, whole],
        out_specs=(whole,) * 8,
        scratch_shapes=[
            vm((3, 4, 2, rows, 2 * tokens), BF16),
            vm((units, 2 * tokens, width), BF16),
            vm((4, ff // 16, 4 * tokens), BF16),
            vm((4 * tokens, width), BF16),
            vm((units, 4, rows, width), BF16),
            vm((units, 4, rows, width), BF16),
            vm((all_units, 4, rows, width), BF16),
            vm((all_units, 4, rows, width), BF16),
            vm((all_units, rows, width), BF16),
            vm((5, 32, width), F32),
            vm((4, 32, width), F32),
            dma((6,)),
            dma((units + 3,)),
            dma((units + 3,)),
            dma((units,)),
            dma((units,)),
            dma((2, 4)),
            dma((2, 4)),
            dma((all_units, 4)),
            dma((all_units, 5)),
            dma((4,)),
            dma((4,)),
        ],
        compiler_params=pltpu.CompilerParams(
            collective_id=1, has_side_effects=True, vmem_limit_bytes=56 * 2**20
        ),
        name="shares",
    )(at_small, at_active, b_all, small)


def plain_shares(at_small, at_active, b_all, small, heads, rels):
    width = at_small.shape[1]
    ff = at_active.shape[0]
    parts = ff // width

    def scattered(left, right):
        grad = jnp.dot(left, right, preferred_element_type=F32)
        return lax.psum_scatter(grad, "batch", scatter_dimension=0, tiled=True)

    def joined(first, count):
        return jnp.concatenate([b_all[first + number] for number in range(count)], axis=1)

    g_fc1 = scattered(at_small[0], joined(0, parts))
    g_qkv = scattered(at_small[1], joined(parts, 3))
    g_out = scattered(at_small[2], b_all[parts + 3])
    g_fc2 = scattered(at_active, b_all[parts + 4])
    small = lax.psum(small, "batch")
    return (
        g_qkv,
        g_out,
        g_fc1,
        g_fc2,
        small[0:4],
        small[4:10],
        small[10:14].reshape(1, ff),
        small[16 : 16 + heads, :rels],
    )


def per_device(
    inputs,
    cotangent,
    segments,
    row_widths,
    w_qkv,
    w_out,
    w_fc1,
    w_fc2,
    norm_gains,
    bias_rows,
    fc1_bias,
    rel_table,
):
    micro, _, slots, width = inputs.shape
    heads, rels = rel_table.shape[1:]
    weights = (w_qkv, w_out, w_fc1, w_fc2, norm_gains, bias_rows, fc1_bias, rel_table)
    activation, grad_in, at_small, at_active, b_all, small = run_block(
        inputs.reshape(micro * slots, width),
        cotangent.reshape(micro * slots, width),
        segments.reshape(micro, slots),
        row_widths.reshape(micro, row_widths.shape[2]),
        weights,
    )
    shares = run_shares if lax.axis_size("batch") == 16 else plain_shares
    grads = shares(at_small, at_active, b_all, small, heads, rels)
    g_qkv, g_out, g_fc1, g_fc2, g_gains, g_biases, g_fc1_bias, g_table = grads
    shape = (1, micro, 1, slots, width)
    return (
        activation.reshape(shape),
        grad_in.reshape(shape),
        g_qkv[None],
        g_out[None],
        g_fc1[None],
        g_fc2[None],
        g_gains[None],
        g_biases[None],
        g_fc1_bias,
        g_table[None],
    )


def solution(mesh):
    return jax.shard_map(
        per_device,
        mesh=mesh,
        in_specs=(
            P(None, "batch", None, None),
            P(None, "batch", None, None),
            P(None, "batch", None),
            P(None, "batch", None),
            P("section", None, None),
            P("section", None, None),
            P("section", None, None),
            P("section", None, None),
            P("section", None, None),
            P("section", None, None),
            P("section", None),
            P("section", None, None),
        ),
        out_specs=(
            P("section", None, "batch", None, None),
            P("section", None, "batch", None, None),
            P("section", "batch", None),
            P("section", "batch", None),
            P("section", "batch", None),
            P("section", "batch", None),
            P("section", None, None),
            P("section", None, None),
            P("section", None),
            P("section", None, None),
        ),
        check_vma=False,
    )
```

time: 1190 us -> 166 us (0.14)
  waiting for transfers between devices: 793 us -> 0 us
  Pallas kernels: 0 us -> 150 us
  other arithmetic: 115 us -> 0 us
  local copies, waits for them, and re-layouts: 128 us -> 14.4 us
  matrix products: 111 us -> 0 us
  between operations: 15.2 us -> 0.71 us
    reduce_scatter x4 -> x0, waiting for transfers between devices: 642 us -> none  [the longest x1 176 us: per_device(): lax.psum_scatter(totals[3], 'batch', scatter_dimension=0, tiled=True)]
    pallas_call x0 -> x2, Pallas kernels: none -> 150 us  [the longest x1 96.1 us: run_shares(): pl.pallas_call(share_kernel, out_shape=(jax.ShapeDtypeStruct((rows, 3 * w...]
    dot_general x46 -> x0, matrix products: 111 us -> none  [the longest x4 19.3 us: forward(): jnp.dot(active, w_fc2, preferred_element_type=jnp.float32) + bias_rows[5]]
    psum x1 -> x0, waiting for transfers between devices: 99.9 us -> none  [per_device(): lax.psum((totals[4], totals[5], totals[6], totals[7]), 'batch')]
    gather x8 -> x0, local copies, waits for them, and re-layouts: 68.8 us -> none  [forward(): pos_bias = jnp.take(pos_table, rel_index, axis=1)]
    ppermute x4 -> x0, waiting for transfers between devices: 49 us -> none  [passed_along(): lax.ppermute(value, axis, [(source, source + steps) for source in range(l...]
    scatter-add x2 -> x0, other arithmetic: 45.6 us -> none  [backward(): jax.ops.segment_sum(head_vals, flat_index, num_segments=rel_count)]
    add x10 -> x0, other arithmetic: 43 us -> none  [fold_in(): left_val + right_val]
  transfers between devices with their start and end apart: 9 -> 0, of which waited for: 6 -> 0; matrix products, arithmetic and copies ran while one was open for 12% -> 0% of each run, Pallas kernels for 0% -> 0%
where the time goes in v1:
time: 166 us; the launch traced here: 165 us
  Pallas kernels  150 us (90%)
  local copies, waits for them, and re-layouts  14.4 us (9%)
    pallas_call x1, Pallas kernels, run_shares(): pl.pallas_call(share_kernel, out_shape=(jax.ShapeDtypeStruct((rows, 3 * w...  96.1 us
    pallas_call x1, Pallas kernels, run_block(): pl.pallas_call(block_kernel, out_shape=(jax.ShapeDtypeStruct((tokens, wid...  54.3 us
    unnamed x22, local copies, waits for them, and re-layouts  14.4 us

profile of v1, /device:TPU:0, one launch (start us, length us, event | category | flops | bytes accessed | tf_op | source)
XLA Modules:
  0.0 165.5 jit_solution(11391505599967624307)
XLA Ops:
  0.6 1.3 copy.22.biases
  2.0 1.4 copy.29
  3.4 54.3 %block.1 = (bf16[128,768]{1,0:T(8,128)(2,1)}, f32[128,768]{1,0:T(8,128)}, bf16[3,768,128]{2,1,0:T(8,128)(2,1)}, bf16[3072,128]{1,0:T(8,128)(2,1)}, bf16[9,128,768]{2,1,0:T(8,128)(2,1)}, /*index=5*/f32[32,768]{1,0:T(8,128)}) custom-call(bf16[128,768]{1,0:T(8,128)(2,1)} %bitcast.28, bf16[128,768]{1,0:T(8,128)(2,1)} %bitcast.29, s32[2,64]{1,0:T(2,128)} %bitcast.36, ...), custom_call_target="tpu_custom_call" | custom-call | tf_op jit(solution)/shard_map/block/pallas_call | solution.py:494
  57.6 0.0 copy-start.2
  57.7 0.0 copy-start.1
  57.7 96.1 %shares.1 = (f32[48,2304]{1,0:T(8,128)}, f32[48,768]{1,0:T(8,128)}, f32[48,3072]{1,0:T(8,128)}, f32[192,768]{1,0:T(8,128)}, f32[4,768]{1,0:T(4,128)}, /*index=5*...) custom-call(bf16[3,4,2,2,48,128]{5,4,3,2,1,0:T(8,128)(2,1)} %bitcast.23, bf16[4,2,2,192,128]{4,3,2,1,0:T(8,128)(2,1)} %bitcast.22, ...), custom_call_target="tpu_custom_call" | custom-call | tf_op jit(solution)/shard_map/shares/pallas_call | solution.py:900
  153.8 0.0 copy-start
  153.8 0.0 copy-start.4
  153.8 0.0 copy-start.3
  153.8 1.4 copy.25
  155.3 1.5 copy.26
  156.7 0.0 copy-done.2
  156.7 0.7 copy.38
  157.4 0.0 copy-done.1
  157.4 0.7 copy.39
  158.1 1.8 %copy.40 = f32[1,48,2304]{2,1,0:T(8,128)} copy(f32[1,48,2304]{2,1,0:T(8,128)} %bitcast.26) | data formatting | bytes 884736
  160.0 1.6 copy.41
  161.5 1.9 %copy.42 = f32[1,48,3072]{2,1,0:T(8,128)} copy(f32[1,48,3072]{2,1,0:T(8,128)} %bitcast.25) | data formatting | bytes 1179648
  163.4 0.0 copy-done
  163.5 0.8 copy.43
  164.3 0.0 copy-done.4
  164.3 0.6 copy.44
  164.9 0.0 copy-done.3
  164.9 0.6 copy.45
Async XLA Ops:
  57.6 99.1 %copy-start.2 = (bf16[128,768]{1,0:T(8,128)(2,1)S(1)}, bf16[128,768]{1,0:T(8,128)(2,1)}, u32[]{:S(2)}) copy-start(bf16[128,768]{1,0:T(8,128)(2,1)} %get-tuple-element.24) | copy-start | bytes 589828
  57.7 99.7 %copy-start.1 = (f32[128,768]{1,0:T(8,128)S(1)}, f32[128,768]{1,0:T(8,128)}, u32[]{:S(2)}) copy-start(f32[128,768]{1,0:T(8,128)} %get-tuple-element.25) | copy-start | bytes 1179652
  153.8 9.6 %copy-start = (f32[192,768]{1,0:T(8,128)S(1)}, f32[192,768]{1,0:T(8,128)}, u32[]{:S(2)}) copy-start(f32[192,768]{1,0:T(8,128)} %get-tuple-element.33) | copy-start | bytes 1769476
  153.8 10.4 %copy-start.4 = (f32[4,768]{1,0:T(4,128)S(1)}, f32[4,768]{1,0:T(4,128)}, u32[]{:S(2)}) copy-start(f32[4,768]{1,0:T(4,128)} %get-tuple-element.34) | copy-start | bytes 36868
  153.8 11.0 %copy-start.3 = (f32[1,3072]{1,0:T(1,128)S(1)}, f32[1,3072]{1,0:T(1,128)}, u32[]{:S(2)}) copy-start(f32[1,3072]{1,0:T(1,128)} %get-tuple-element.66) | copy-start | bytes 36868

commit v2 on v1

--- a/solution.py
+++ b/solution.py
@@ -68,7 +68,7 @@
         body(index)
         return carry
 
-    lax.fori_loop(0, count, step, 0)
+    lax.fori_loop(0, count, step, 0, unroll=True)
 
 
 def cols_of(index, size=COLS):
@@ -124,9 +124,10 @@
 
 
 def spread_table(table, padded, spread, wide_table):
-    heads, rels = table.shape
+    heads, _, rels = table.shape
     padded[...] = jnp.zeros_like(padded)
-    padded[0:heads, 0:rels] = table[...]
+    for head in range(heads):
+        padded[head : head + 1, 0:rels] = table[head]
     shape = spread.shape
     where = iota((1, WIDE), 1)
     signed = jnp.where(where < HALF, where, where - WIDE)
@@ -303,7 +304,7 @@
             out = nn(normed[...], wqkv[:, cols_of(third * per_part + index)])
             if third != 1:
                 row = 1 if third == 0 else 2
-                out = out + biases[0, row : row + 1, cols_of(index)]
+                out = out + biases[row, 0:1, cols_of(index)]
             qkv[third, :, cols_of(index)] = out.astype(BF16)
 
         chunk_loop(per_part, project)
@@ -333,7 +334,7 @@
 
     def attend_out(index):
         at = cols_of(index)
-        out = nn(mixed[...], wout[:, at]) + biases[0, 3:4, at]
+        out = nn(mixed[...], wout[:, at]) + biases[3, 0:1, at]
         att_out[:, at] = out
         stream[:, at] = stream[:, at] + gains[0, 1:2, at] * out
 
@@ -341,7 +342,7 @@
     hat, inv_scale = norm_parts(stream[...])
     hat_two[...] = hat
     scale_two[...] = inv_scale
-    second[...] = (hat * gains[0, 2:3, :] + biases[0, 4:5, :]).astype(BF16)
+    second[...] = (hat * gains[0, 2:3, :] + biases[4, 0:1, :]).astype(BF16)
     loads[2].wait()
 
     def feed(index):
@@ -357,7 +358,7 @@
 
     def feed_out(index):
         at = cols_of(index)
-        out = nn(active[...], wfc2[:, at]) + biases[0, 5:6, at]
+        out = nn(active[...], wfc2[:, at]) + biases[5, 0:1, at]
         branch[:, at] = out
         activation[:, at] = (stream[:, at] + gains[0, 3:4, at] * out).astype(BF16)
 
@@ -485,7 +486,8 @@
     w_qkv, w_out, w_fc1, w_fc2, gains, biases, fc1_bias, table = weights
     tokens, width = inputs.shape
     ff = w_fc1.shape[2]
-    heads, rels = table.shape[1:]
+    heads = table.shape[1]
+    rels = table.shape[2]
     parts = ff // width
     cells = GRID_ROWS * GRID_COLS
     whole = pl.BlockSpec(memory_space=pltpu.VMEM)
@@ -543,9 +545,11 @@
             collective_id=0, has_side_effects=True, vmem_limit_bytes=56 * 2**20
         ),
         name="block",
-    )(inputs, cotangent, seg, wid, w_qkv, w_out, w_fc1, w_fc2, gains, biases, fc1_bias, table[0])
-
-
+    )(inputs, cotangent, seg, wid, w_qkv, w_out, w_fc1, w_fc2, gains, jnp.swapaxes(biases, 0, 1), fc1_bias, jnp.swapaxes(table, 0, 1))
+
+
+AHEAD = 3
+DEPTHS = (2, 4, 6, 8)
 UNIT_LEFT = (0, 0, 0, 0, 1, 1, 1, 2)
 
 
@@ -715,23 +719,30 @@
         )
         for step in range(4)
     ]
+    queue = [
+        [x_left[0], x_right[0]],
+        [x_right[1]],
+        [x_right[2]],
+        list(four[4:6]),
+        [x_right[3]],
+        list(four[0:2]),
+        [x_left[1], x_right[4]],
+        [x_right[5]],
+        [x_right[6]],
+        [x_left[2], x_right[7]],
+    ]
+
+    def issue(count):
+        for _ in range(count):
+            if queue:
+                for copy in queue.pop(0):
+                    copy.start()
+
     small_copy[0].start()
-    x_left[0].start()
-    x_right[0].start()
+    issue(1)
     for copy in four[2:4]:
         copy.start()
-    x_right[1].start()
-    for copy in four[4:6]:
-        copy.start()
-    x_right[2].start()
-    x_right[3].start()
-    for copy in four[0:2]:
-        copy.start()
-    x_left[1].start()
-    for unit in (4, 5, 6):
-        x_right[unit].start()
-    x_left[2].start()
-    x_right[7].start()
+    issue(AHEAD)
 
     y_copy = [
         remote(
@@ -758,11 +769,13 @@
                 waited.add("four")
                 for copy in four:
                     copy.wait_recv()
+            issue(1)
             return
         if UNIT_LEFT[unit] not in waited:
             waited.add(UNIT_LEFT[unit])
             x_left[UNIT_LEFT[unit]].wait_recv()
         x_right[unit].wait_recv()
+        issue(1)
         y_send[unit] = product(unit, 1 - y).astype(BF16).reshape(4, rows, width)
         y_copy[unit].start()
 
@@ -850,12 +863,12 @@
         if step < 3:
             small_copy[step + 1].start()
 
-    stages = (first, second, third, fourth, fifth)
-    for turn in range(len(order) + len(stages) - 1):
-        for depth in (0, 1, 2, 3, 4):
+    stages = ((first, 0), (second, DEPTHS[0]), (third, DEPTHS[1]), (fourth, DEPTHS[2]), (fifth, DEPTHS[3]))
+    for turn in range(len(order) + DEPTHS[3]):
+        for stage, depth in stages:
             index = turn - depth
             if 0 <= index < len(order):
-                stages[depth](order[index])
+                stage(order[index])
         if turn < 4:
             small_step(turn)
 
@@ -971,6 +984,33 @@
     )
 
 
+def finish_kernel(count, *refs):
+    for source, target in zip(refs[:count], refs[count:]):
+        if source.shape == target.shape:
+            target[...] = source[...]
+        else:
+            for row in range(target.shape[0]):
+                target[row] = source[row : row + 1, :]
+
+
+def finish(plain, spaced):
+    shapes = [array.shape for array in plain] + [
+        (array.shape[0], 1, array.shape[1]) for array in spaced
+    ]
+    arrays = list(plain) + list(spaced)
+    whole = pl.BlockSpec(memory_space=pltpu.VMEM)
+    return pl.pallas_call(
+        functools.partial(finish_kernel, len(arrays)),
+        out_shape=tuple(
+            jax.ShapeDtypeStruct(shape, array.dtype) for shape, array in zip(shapes, arrays)
+        ),
+        in_specs=[whole] * len(arrays),
+        out_specs=(whole,) * len(arrays),
+        compiler_params=pltpu.CompilerParams(vmem_limit_bytes=24 * 2**20),
+        name="finish",
+    )(*arrays)
+
+
 def per_device(
     inputs,
     cotangent,
@@ -998,6 +1038,9 @@
     shares = run_shares if lax.axis_size("batch") == 16 else plain_shares
     grads = shares(at_small, at_active, b_all, small, heads, rels)
     g_qkv, g_out, g_fc1, g_fc2, g_gains, g_biases, g_fc1_bias, g_table = grads
+    activation, grad_in, g_qkv, g_out, g_fc1, g_fc2, g_gains, g_fc1_bias, g_biases, g_table = finish(
+        (activation, grad_in, g_qkv, g_out, g_fc1, g_fc2, g_gains, g_fc1_bias), (g_biases, g_table)
+    )
     shape = (1, micro, 1, slots, width)
     return (
         activation.reshape(shape),
@@ -1007,9 +1050,9 @@
         g_fc1[None],
         g_fc2[None],
         g_gains[None],
-        g_biases[None],
+        jnp.swapaxes(g_biases, 0, 1),
         g_fc1_bias,
-        g_table[None],
+        jnp.swapaxes(g_table, 0, 1),
     )
 
 

time: 166 us -> 141 us (0.85)
  Pallas kernels: 150 us -> 132 us
  local copies, waits for them, and re-layouts: 14.4 us -> 7.92 us
    pallas_call x1, Pallas kernels: 54.3 us -> 36.7 us  [run_block(): pl.pallas_call(block_kernel, out_shape=(jax.ShapeDtypeStruct((tokens, wid...]
    unnamed x22 -> x20, local copies, waits for them, and re-layouts: 14.4 us -> 7.92 us
    pallas_call x1, Pallas kernels: 96.1 us -> 94.1 us  [run_shares(): pl.pallas_call(share_kernel, out_shape=(jax.ShapeDtypeStruct((rows, 3 * w...]
where the time goes in v2:
time: 141 us
  Pallas kernels  132 us (94%)
  local copies, waits for them, and re-layouts  7.92 us (6%)
    pallas_call x1, Pallas kernels, run_shares(): pl.pallas_call(share_kernel, out_shape=(jax.ShapeDtypeStruct((rows, 3 * w...  94.1 us
    pallas_call x1, Pallas kernels, run_block(): pl.pallas_call(block_kernel, out_shape=(jax.ShapeDtypeStruct((tokens, wid...  36.7 us
    unnamed x20, local copies, waits for them, and re-layouts  7.92 us

profile of v2, /device:TPU:0, one launch (start us, length us, event | category | flops | bytes accessed | tf_op | source)
XLA Modules:
  0.0 140.9 jit_solution(17174818988221525309)
XLA Ops:
  0.6 36.7 %block.1 = (bf16[128,768]{1,0:T(8,128)(2,1)}, f32[128,768]{1,0:T(8,128)}, bf16[3,768,128]{2,1,0:T(8,128)(2,1)}, bf16[3072,128]{1,0:T(8,128)(2,1)}, bf16[9,128,768]{2,1,0:T(8,128)(2,1)}, /*index=5*/f32[32,768]{1,0:T(8,128)}) custom-call(bf16[128,768]{1,0:T(8,128)(2,1)} %bitcast.23, bf16[128,768]{1,0:T(8,128)(2,1)} %bitcast.24, s32[2,64]{1,0:T(2,128)} %bitcast.27, ...), custom_call_target="tpu_custom_call" | custom-call | tf_op jit(solution)/shard_map/block/pallas_call | solution.py:496
  37.3 0.0 copy-start.3
  37.4 94.1 %shares.1 = (f32[48,2304]{1,0:T(8,128)}, f32[48,768]{1,0:T(8,128)}, f32[48,3072]{1,0:T(8,128)}, f32[192,768]{1,0:T(8,128)}, f32[4,768]{1,0:T(4,128)}, /*index=5*...) custom-call(bf16[3,4,2,2,48,128]{5,4,3,2,1,0:T(8,128)(2,1)} %bitcast.22, bf16[4,2,2,192,128]{4,3,2,1,0:T(8,128)(2,1)} %bitcast.21, ...), custom_call_target="tpu_custom_call" | custom-call | tf_op jit(solution)/shard_map/shares/pallas_call | solution.py:913
  131.4 0.0 copy-done.3
  131.4 0.0 copy-start
  131.4 1.1 copy-done
  132.5 0.0 copy-start.1
  132.5 1.1 copy-done.1
  133.6 0.0 copy-start.2
  133.6 1.0 copy-done.2
  134.6 0.0 copy-start.4
  134.6 0.9 copy-done.4
  135.5 0.0 copy-start.5
  135.5 0.9 copy-done.5
  136.4 0.0 copy-start.6
  136.4 0.8 copy-done.6
  137.2 0.0 copy-start.7
  137.2 0.7 copy-done.7
  137.9 0.0 copy-start.8
  137.9 0.7 copy-done.8
  138.6 0.0 copy-start.9
  138.6 0.7 copy-done.9
  139.4 1.6 %finish.1 = (bf16[128,768]{1,0:T(8,128)(2,1)}, f32[128,768]{1,0:T(8,128)}, f32[48,2304]{1,0:T(8,128)}, f32[48,768]{1,0:T(8,128)}, f32[48,3072]{1,0:T(8,128)}, /*...) custom-call(bf16[128,768]{1,0:T(8,128)(2,1)S(1)} %copy-done.4, ...), custom_call_target="tpu_custom_call" | custom-call | tf_op jit(solution)/shard_map/finish/pallas_call | solution.py:1002
Async XLA Ops:
  37.3 94.1 %copy-start.3 = (f32[128,768]{1,0:T(8,128)S(1)}, f32[128,768]{1,0:T(8,128)}, u32[]{:S(2)}) copy-start(f32[128,768]{1,0:T(8,128)} %get-tuple-element.35.refs_1_) | copy-start | bytes 1179652
  131.4 1.1 copy-start
  132.5 1.1 copy-start.1
  133.6 1.0 copy-start.2
  134.6 0.9 copy-start.4
  135.5 0.9 copy-start.5
  136.4 0.8 copy-start.6
  137.2 0.7 copy-start.7
  137.9 0.7 copy-start.8
  138.6 0.7 copy-start.9

commit v3 on v1

v3 whole, which is shorter than its diff:
```python
import functools

import jax
import jax.numpy as jnp
from jax import lax
from jax.experimental import pallas as pl
from jax.experimental.pallas import tpu as pltpu
from jax.sharding import PartitionSpec as P

MESH = pl.DeviceIdType.MESH
F32 = jnp.float32
BF16 = jnp.bfloat16
REACH = 13
SPAN = 2 * REACH + 1
NORM_EPS = 1e-06
ROOT_HALF = 0.7071067811865476
INV_ROOT_TWO_PI = 0.3989422804014327
COLS = 256
GRID_ROWS = 8
GRID_COLS = 16
PITCH = 2 * GRID_COLS
WIDE = 2 * GRID_ROWS * PITCH
HALF = WIDE // 2


def nn(left, right):
    return lax.dot_general(left, right, (((1,), (0,)), ((), ())), preferred_element_type=F32)


def nt(left, right):
    return lax.dot_general(left, right, (((1,), (1,)), ((), ())), preferred_element_type=F32)


def tn(left, right):
    return lax.dot_general(left, right, (((0,), (0,)), ((), ())), preferred_element_type=F32)


def iota(shape, dim):
    return lax.broadcasted_iota(jnp.int32, shape, dim)


def two_parts(value):
    high = value.astype(BF16)
    return high, (value - high.astype(F32)).astype(BF16)


def norm_parts(values_in):
    row_mean = jnp.mean(values_in, axis=-1, keepdims=True)
    centered = values_in - row_mean
    inv_scale = lax.rsqrt(jnp.mean(centered * centered, axis=-1, keepdims=True) + NORM_EPS)
    return centered * inv_scale, inv_scale


def norm_back(upstream, normal_in, inv_scale):
    return inv_scale * (
        upstream
        - jnp.mean(upstream, axis=-1, keepdims=True)
        - normal_in * jnp.mean(upstream * normal_in, axis=-1, keepdims=True)
    )


def col_sum(value):
    return jnp.sum(value, axis=0, keepdims=True)


def cols_of(index, size=COLS):
    return slice(index * size, (index + 1) * size)


def geometry(seg, wid, same, pick_q, pick_k, pick_kt, pick_qt):
    micro, slots = seg.shape
    tokens = micro * slots
    images = wid.shape[1]
    seg_f = seg[...].astype(F32)
    seg_row = jnp.concatenate(
        [seg_f[m : m + 1, :] + float(m * images) for m in range(micro)], axis=1
    )
    sub = iota((tokens, tokens), 0)
    lane = iota((tokens, tokens), 1)
    seg_col = jnp.sum(jnp.where(sub == lane, seg_row, 0.0), axis=1, keepdims=True)
    same[...] = (seg_col == seg_row).astype(F32)
    before_row = jnp.sum((seg_col < seg_row).astype(F32), axis=0, keepdims=True)
    before_col = jnp.sum((seg_row < seg_col).astype(F32), axis=1, keepdims=True)
    place_row = iota((1, tokens), 1).astype(F32) - before_row
    place_col = iota((tokens, 1), 0).astype(F32) - before_col
    width_row = jnp.zeros((1, tokens), F32)
    width_col = jnp.zeros((tokens, 1), F32)
    for m in range(micro):
        for image in range(images):
            width = wid[m, image].astype(F32)
            number = float(m * images + image)
            width_row = width_row + jnp.where(seg_row == number, width, 0.0)
            width_col = width_col + jnp.where(seg_col == number, width, 0.0)

    def grid(place, width):
        row = jnp.zeros_like(place)
        for k in range(1, GRID_ROWS):
            row = row + (place >= float(k) * width).astype(F32)
        return row, place - row * width

    row_r, col_r = grid(place_row, width_row)
    row_c, col_c = grid(place_col, width_col)
    cells = GRID_ROWS * GRID_COLS
    pick_q[...] = (iota((tokens, cells), 1).astype(F32) == row_c * GRID_COLS + col_c).astype(
        F32
    ).astype(BF16)
    pick_qt[...] = (
        iota((cells, tokens), 0).astype(F32) == row_r * GRID_COLS + (GRID_COLS - 1.0) - col_r
    ).astype(F32).astype(BF16)
    pick_k[...] = (iota((tokens, HALF), 1).astype(F32) == row_c * PITCH + col_c).astype(
        F32
    ).astype(BF16)
    pick_kt[...] = (iota((HALF, tokens), 0).astype(F32) == row_r * PITCH + col_r).astype(
        F32
    ).astype(BF16)


def spread_table(table, padded, spread, wide_table):
    heads, _, rels = table.shape
    padded[...] = jnp.zeros_like(padded)
    for head in range(heads):
        padded[head : head + 1, 0:rels] = table[head]
    shape = spread.shape
    where = iota((1, WIDE), 1)
    signed = jnp.where(where < HALF, where, where - WIDE)
    row_step = (signed + GRID_COLS + WIDE) // PITCH - WIDE // PITCH
    col_step = signed - row_step * PITCH
    entry = (REACH - row_step) * SPAN + jnp.clip(-col_step, -REACH, REACH) + REACH
    spread[...] = (iota(shape, 0) == entry).astype(F32).astype(BF16)
    high, low = two_parts(padded[...])
    vector = nn(high, spread[...]) + nn(low, spread[...])
    cells = GRID_ROWS * GRID_COLS
    for head in range(heads):
        line = jnp.broadcast_to(vector[head : head + 1, :], (GRID_COLS, WIDE))
        line = pltpu.roll(line, 0, 1, stride=1, stride_axis=0)
        for low_row in range(4):
            turned = line if low_row == 0 else pltpu.roll(line, low_row * PITCH, 1)
            for high_row in range(GRID_ROWS // 4):
                if high_row == 0:
                    part = turned[:, 0:HALF]
                else:
                    part = jnp.concatenate(
                        [turned[:, WIDE - 4 * PITCH : WIDE], turned[:, 0 : HALF - 4 * PITCH]], axis=1
                    )
                top = (high_row * 4 + low_row) * GRID_COLS
                part_high, part_low = two_parts(part)
                wide_table[top : top + GRID_COLS, head * HALF : (head + 1) * HALF] = part_high
                wide_table[
                    cells + top : cells + top + GRID_COLS, head * HALF : (head + 1) * HALF
                ] = part_low


def fold_table(head_grad):
    total = None
    for low_row in range(4):
        near = head_grad[low_row * GRID_COLS : (low_row + 1) * GRID_COLS, :]
        far = head_grad[(low_row + 4) * GRID_COLS : (low_row + 5) * GRID_COLS, :]
        step = 4 * PITCH
        laid = jnp.concatenate(
            [
                near[:, 0:step] + far[:, step : 2 * step],
                near[:, step : 2 * step],
                jnp.zeros((GRID_COLS, step), F32),
                far[:, 0:step],
            ],
            axis=1,
        )
        if low_row > 0:
            laid = pltpu.roll(laid, WIDE - low_row * PITCH, 1)
        total = laid if total is None else total + laid
    total = pltpu.roll(total, WIDE - (GRID_COLS - 1), 1, stride=1, stride_axis=0)
    return col_sum(total)


def block_body(
    hooks,
    at_small,
    at_active,
    b_at,
    inputs,
    cotangent,
    seg,
    wid,
    wqkv_in,
    wout_in,
    wfc1_in,
    wfc2_in,
    gains,
    biases,
    fc1_bias,
    table,
    activation,
    grad_in,
    small,
    wqkv,
    wout,
    wfc1,
    wfc2,
    arrived,
    leaving,
    stream,
    hat_one,
    hat_two,
    att_out,
    branch,
    d_middle,
    d_wide,
    normed,
    qkv,
    probs,
    bias,
    mixed,
    d_mixed,
    second,
    active,
    slope,
    same,
    pick_q,
    pick_k,
    pick_kt,
    pick_qt,
    padded,
    spread,
    wide_table,
    folded,
    scale_one,
    scale_two,
    weight_sem,
    send_sem,
    recv_sem,
):
    section = lax.axis_index("section")
    place = lax.axis_index("batch")
    other = (1 - section, place)
    width = inputs.shape[1]
    tokens = inputs.shape[0]
    ff = active.shape[1]
    heads = table.shape[0]
    pair = 2 * (width // heads)
    pairs = heads // 2
    parts = ff // width
    per_part = width // COLS

    loads = [
        pltpu.make_async_copy(source.at[0], target, weight_sem.at[index])
        for index, (source, target) in enumerate(
            [(wqkv_in, wqkv), (wout_in, wout), (wfc1_in, wfc1), (wfc2_in, wfc2)]
        )
    ]
    for load in loads:
        load.start()

    hooks.greet(other)

    geometry(seg, wid, same, pick_q, pick_k, pick_kt, pick_qt)
    spread_table(table, padded, spread, wide_table)
    cells = GRID_ROWS * GRID_COLS

    def bias_of(head):
        where = cols_of(head, HALF)
        high = nn(pick_q[...], wide_table[0:cells, where]).astype(BF16)
        low = nn(pick_q[...], wide_table[cells : 2 * cells, where]).astype(BF16)
        bias[cols_of(head, tokens), :] = nn(high, pick_kt[...]) + nn(low, pick_kt[...])

    for index in range(heads):
        bias_of(index)

    hooks.met()

    def relay(source):
        return pltpu.make_async_remote_copy(
            src_ref=source,
            dst_ref=arrived,
            send_sem=send_sem,
            recv_sem=recv_sem,
            device_id=other,
            device_id_type=MESH,
        )

    @pl.when(section == 0)
    def _():
        stream[...] = inputs[...].astype(F32)

    @pl.when(section == 1)
    def _():
        relay(activation).wait_recv()
        stream[...] = arrived[...].astype(F32)

    def turn_small(number, source):
        at_small[number] = source[...].T.reshape(at_small.shape[1:])

    hat, inv_scale = norm_parts(stream[...])
    hat_one[...] = hat
    scale_one[...] = inv_scale
    normed[...] = (hat * gains[0, 0:1, :] + biases[0, 0:1, :]).astype(BF16)
    turn_small(1, normed)
    loads[0].wait()
    for third in range(3):

        def project(index):
            out = nn(normed[...], wqkv[:, cols_of(third * per_part + index)])
            if third != 1:
                row = 1 if third == 0 else 2
                out = out + biases[row, 0:1, cols_of(index)]
            qkv[third, :, cols_of(index)] = out.astype(BF16)

        for index in range(per_part):
            project(index)

    lane = iota((1, pair), 1)
    low_lanes = (lane < pair // 2).astype(F32).astype(BF16)
    high_lanes = (lane >= pair // 2).astype(F32).astype(BF16)

    def stacked(value):
        return jnp.concatenate([value * low_lanes, value * high_lanes], axis=0)

    def side_by_side(value):
        return jnp.concatenate([value[0:tokens, :], value[tokens : 2 * tokens, :]], axis=1)

    for index in range(pairs):
        at = slice(index * pair, (index + 1) * pair)
        rows = slice(index * 2 * tokens, (index + 1) * 2 * tokens)
        raw = nt(stacked(qkv[0, :, at]), qkv[1, :, at])
        mask = jnp.concatenate([same[...], same[...]], axis=0) > 0.5
        scores = jnp.where(mask, raw * 0.125 + bias[rows, :], -1e30)
        exped = jnp.exp(scores - jnp.max(scores, axis=-1, keepdims=True))
        prob = exped / jnp.sum(exped, axis=-1, keepdims=True)
        probs[rows, :] = prob
        mixed[:, at] = nn(side_by_side(prob.astype(BF16)), stacked(qkv[2, :, at])).astype(BF16)

    turn_small(2, mixed)
    loads[1].wait()

    def attend_out(index):
        at = cols_of(index)
        out = nn(mixed[...], wout[:, at]) + biases[3, 0:1, at]
        att_out[:, at] = out
        stream[:, at] = stream[:, at] + gains[0, 1:2, at] * out

    for index in range(per_part):
        attend_out(index)
    hat, inv_scale = norm_parts(stream[...])
    hat_two[...] = hat
    scale_two[...] = inv_scale
    second[...] = (hat * gains[0, 2:3, :] + biases[4, 0:1, :]).astype(BF16)
    turn_small(0, second)
    loads[2].wait()

    def feed(index):
        at = cols_of(index)
        hidden = nn(second[...], wfc1[:, at]) + fc1_bias[0:1, at]
        cumul = 0.5 * (1.0 + lax.erf(hidden * ROOT_HALF))
        density = jnp.exp(-0.5 * hidden * hidden) * INV_ROOT_TWO_PI
        active[:, at] = (hidden * cumul).astype(BF16)
        slope[:, at] = cumul + hidden * density
        if (index + 1) % per_part == 0:
            part = index // per_part
            at_active[part] = active[:, cols_of(part, width)].T.reshape(at_active.shape[1:])

    for index in range(ff // COLS):
        feed(index)
    loads[3].wait()

    def feed_out(index):
        at = cols_of(index)
        out = nn(active[...], wfc2[:, at]) + biases[5, 0:1, at]
        branch[:, at] = out
        activation[:, at] = (stream[:, at] + gains[0, 3:4, at] * out).astype(BF16)

    for index in range(per_part):
        feed_out(index)

    @pl.when(section == 0)
    def _():
        relay(activation).start()

    hooks.forward_done()

    @pl.when(section == 0)
    def _():
        relay(activation).wait_send()
        relay(activation).wait_recv()
        stream[...] = arrived[...].astype(F32)

    @pl.when(section == 1)
    def _():
        stream[...] = cotangent[...].astype(F32)

    small[...] = jnp.zeros_like(small)
    upstream = stream[...]
    small[3:4, :] = col_sum(upstream * branch[...])
    d_branch = (gains[0, 3:4, :] * upstream).astype(BF16)
    b_at(parts + 4)[...] = d_branch
    small[9:10, :] = col_sum(d_branch.astype(F32))
    hooks.branch_done()

    def feed_back(index):
        at = cols_of(index)
        out = nt(b_at(parts + 4)[...], wfc2[at, :])
        d_hidden = (out * slope[:, at]).astype(BF16)
        part = index // per_part
        inner = cols_of(index % per_part)
        b_at(part)[:, inner] = d_hidden
        small[10 + part : 11 + part, inner] = col_sum(d_hidden.astype(F32))
        if (index + 1) % per_part == 0:
            hooks.hidden_done(part)

    for index in range(ff // COLS):
        feed_back(index)

    def second_back(index):
        at = cols_of(index)
        out = nt(b_at(0)[...], wfc1[at, 0:width])
        for part in range(1, parts):
            out = out + nt(b_at(part)[...], wfc1[at, part * width : (part + 1) * width])
        d_wide[:, at] = out

    for index in range(per_part):
        second_back(index)
    d_second = d_wide[...]
    small[2:3, :] = col_sum(d_second * hat_two[...])
    small[8:9, :] = col_sum(d_second)
    d_mid = stream[...] + norm_back(d_second * gains[0, 2:3, :], hat_two[...], scale_two[...])
    d_middle[...] = d_mid
    small[1:2, :] = col_sum(d_mid * att_out[...])
    d_att = (gains[0, 1:2, :] * d_mid).astype(BF16)
    b_at(parts + 3)[...] = d_att
    small[7:8, :] = col_sum(d_att.astype(F32))
    hooks.attention_out_done()

    def out_back(index):
        at = cols_of(index)
        d_mixed[:, at] = nt(b_at(parts + 3)[...], wout[at, :]).astype(BF16)

    for index in range(per_part):
        out_back(index)

    hooks.attention_next()
    folded[...] = jnp.zeros_like(folded)
    for index in range(pairs):
        at = slice(index * pair, (index + 1) * pair)
        rows = slice(index * 2 * tokens, (index + 1) * 2 * tokens)
        prob = probs[rows, :]
        d_mix = stacked(d_mixed[:, at])
        d_prob = nt(d_mix, qkv[2, :, at])
        b_at(parts + 2)[:, at] = tn(prob.astype(BF16), d_mix).astype(BF16)
        d_scores = prob * (d_prob - jnp.sum(prob * d_prob, axis=-1, keepdims=True))
        d_raw = (0.125 * d_scores).astype(BF16)
        b_at(parts)[:, at] = nn(side_by_side(d_raw), stacked(qkv[1, :, at])).astype(BF16)
        b_at(parts + 1)[:, at] = tn(d_raw, stacked(qkv[0, :, at])).astype(BF16)
        high, low = two_parts(d_scores)
        high = nn(high, pick_k[...]).astype(BF16)
        low = nn(low, pick_k[...]).astype(BF16)
        for side in range(2):
            own = slice(side * tokens, (side + 1) * tokens)
            head_grad = nn(pick_qt[...], high[own, :]) + nn(pick_qt[...], low[own, :])
            folded[2 * index + side : 2 * index + side + 1, :] = fold_table(head_grad)

    hooks.qkv_done()
    small[5:6, :] = col_sum(b_at(parts)[...].astype(F32))
    small[6:7, :] = col_sum(b_at(parts + 2)[...].astype(F32))

    def normed_back(index):
        at = cols_of(index)
        out = nt(b_at(parts)[...], wqkv[at, 0:width])
        for third in range(1, 3):
            out = out + nt(b_at(parts + third)[...], wqkv[at, third * width : (third + 1) * width])
        d_wide[:, at] = out

    for index in range(per_part):
        normed_back(index)
    d_normed = d_wide[...]
    small[0:1, :] = col_sum(d_normed * hat_one[...])
    small[4:5, :] = col_sum(d_normed)
    d_in = d_middle[...] + norm_back(d_normed * gains[0, 0:1, :], hat_one[...], scale_one[...])
    grad_in[...] = d_in
    leaving[...] = d_in.astype(BF16)

    @pl.when(section == 1)
    def _():
        relay(leaving).start()

    high, low = two_parts(folded[...])
    small[16:32, :] = nt(high, spread[...]) + nt(low, spread[...])
    hooks.small_done()

    @pl.when(section == 1)
    def _():
        relay(leaving).wait_send()


class Alone:
    def greet(self, other):
        pl.semaphore_signal(
            pltpu.get_barrier_semaphore(), inc=1, device_id=other, device_id_type=MESH
        )

    def met(self):
        pl.semaphore_wait(pltpu.get_barrier_semaphore(), 1)

    def nothing(self, *_):
        pass

    forward_done = branch_done = hidden_done = attention_out_done = nothing
    attention_next = qkv_done = small_done = nothing


def block_kernel(*refs):
    given, (activation, grad_in, at_small, at_active, b_all, small), rest = (
        refs[:12],
        refs[12:18],
        refs[18:],
    )
    block_body(
        Alone(), at_small, at_active, lambda k: b_all.at[k], *given, activation, grad_in, small, *rest
    )


def block_specs():
    whole = pl.BlockSpec(memory_space=pltpu.VMEM)
    return (
        [whole, whole, whole, pl.BlockSpec(memory_space=pltpu.SMEM)]
        + [pl.BlockSpec(memory_space=pl.ANY)] * 4
        + [whole] * 4
    )


def block_scratch(tokens, width, ff, heads, rels):
    cells = GRID_ROWS * GRID_COLS
    padded_rels = -(-rels // 256) * 256
    vm = pltpu.VMEM
    return (
        [
            vm((width, 3 * width), BF16),
            vm((width, width), BF16),
            vm((width, ff), BF16),
            vm((ff, width), BF16),
            vm((tokens, width), BF16),
            vm((tokens, width), BF16),
        ]
        + [vm((tokens, width), F32)] * 7
        + [
            vm((tokens, width), BF16),
            vm((3, tokens, width), BF16),
            vm((heads * tokens, tokens), F32),
            vm((heads * tokens, tokens), F32),
            vm((tokens, width), BF16),
            vm((tokens, width), BF16),
            vm((tokens, width), BF16),
            vm((tokens, ff), BF16),
            vm((tokens, ff), F32),
            vm((tokens, tokens), F32),
            vm((tokens, cells), BF16),
            vm((tokens, HALF), BF16),
            vm((HALF, tokens), BF16),
            vm((cells, tokens), BF16),
            vm((16, padded_rels), F32),
            vm((padded_rels, WIDE), BF16),
            vm((2 * cells, heads * HALF), BF16),
            vm((16, WIDE), F32),
            vm((tokens, 1), F32),
            vm((tokens, 1), F32),
            pltpu.SemaphoreType.DMA((4,)),
            pltpu.SemaphoreType.DMA,
            pltpu.SemaphoreType.DMA,
        ]
    )


N_BLOCK_SCRATCH = 36
UNIT_LEFT = (0, 0, 0, 0, 1, 1, 1, 2)
UNITS = len(UNIT_LEFT)
FOUR_UNITS = 4
EARLY = ((0, 1), (2, 3))
FIRST_ORDER = (7, 4, 5, 6)
SECOND_ORDER = (8, 9, 0, 1, 10, 2, 3, 11, 7, 4, 5, 6)
DEPTHS = (2, 3, 5)


def whole_kernel(*refs):
    given, (activation, grad_in, g_all, small_sum), rest = refs[:12], refs[12:16], refs[16:]
    block_scratches = rest[:N_BLOCK_SCRATCH]
    (
        at_small,
        at_active,
        left,
        right,
        left_four,
        right_four,
        y_send,
        y_recv,
        totals,
        passing,
        inward,
        small_own,
        small_recv,
        own_sem,
        x_send_sem,
        x_recv_sem,
        y_send_sem,
        y_recv_sem,
        four_send_sem,
        four_recv_sem,
        z_send_sem,
        z_recv_sem,
        small_send_sem,
        small_recv_sem,
    ) = rest[N_BLOCK_SCRATCH:]
    section = lax.axis_index("section")
    place = lax.axis_index("batch")
    z = place // 4
    y = (place // 2) % 2
    x = place % 2
    x_peer = z * 4 + y * 2 + (1 - x)
    y_peer = z * 4 + (1 - y) * 2 + x
    xy_peer = z * 4 + (1 - y) * 2 + (1 - x)
    at_end = (z == 0) | (z == 3)
    between = jnp.logical_not(at_end)
    lower = z < 2
    in_peer = jnp.where(lower, place + 4, place - 4)
    out_peer = jnp.where(at_end, place, jnp.where(z == 1, place - 4, place + 4))
    far_peer = jnp.where(lower, place + 8, place - 8)
    pair_peer = jnp.where(z % 2 == 0, place + 4, place - 4)
    tokens = given[0].shape[0]
    rows = left.shape[3]
    width = right.shape[2]
    barrier = pltpu.get_barrier_semaphore()

    def remote(source, target, send, recv, peer):
        return pltpu.make_async_remote_copy(
            src_ref=source,
            dst_ref=target,
            send_sem=send,
            recv_sem=recv,
            device_id=(section, peer),
            device_id_type=MESH,
        )

    own = [
        pltpu.make_async_copy(
            at_small.at[number, :, :, x], left.at[number, :, :, :, 0:tokens], own_sem.at[number]
        )
        for number in range(3)
    ] + [pltpu.make_async_copy(at_active.at[:, y, x], left_four.at[:, :, 0:tokens], own_sem.at[3])]

    others = ((1, y, 1 - x, x_peer), (2, 1 - y, x, y_peer), (3, 1 - y, 1 - x, xy_peer))
    four_left = [
        remote(
            at_active.at[:, peer_y, peer_x],
            left_four.at[:, :, slot * tokens : (slot + 1) * tokens],
            four_send_sem.at[0, slot],
            four_recv_sem.at[0, slot],
            peer,
        )
        for slot, peer_y, peer_x, peer in others
    ]
    four_right = [
        remote(
            right_four.at[0:tokens, :],
            right_four.at[slot * tokens : (slot + 1) * tokens, :],
            four_send_sem.at[1, slot],
            four_recv_sem.at[1, slot],
            peer,
        )
        for slot, _, _, peer in others
    ]
    x_left = [
        remote(
            at_small.at[number, :, :, 1 - x],
            left.at[number, :, :, :, tokens : 2 * tokens],
            x_send_sem.at[UNITS + number],
            x_recv_sem.at[UNITS + number],
            x_peer,
        )
        for number in range(3)
    ]
    x_right = [
        remote(
            right.at[unit, 0:tokens, :],
            right.at[unit, tokens : 2 * tokens, :],
            x_send_sem.at[unit],
            x_recv_sem.at[unit],
            x_peer,
        )
        for unit in range(UNITS)
    ]
    y_copy = [
        remote(
            y_send.at[unit], y_recv.at[unit], y_send_sem.at[unit], y_recv_sem.at[unit], y_peer
        )
        for unit in range(UNITS)
    ]
    small_copy = [
        remote(
            small_own.at[step],
            small_recv.at[step],
            small_send_sem.at[step],
            small_recv_sem.at[step],
            peer,
        )
        for step, peer in enumerate((x_peer, y_peer, pair_peer, far_peer))
    ]

    def start(copies):
        for copy in copies:
            copy.start()

    waited = set()

    def once(name, copies):
        if name not in waited:
            waited.add(name)
            for copy in copies:
                copy.wait_recv()

    def own_ready(number):
        if ("own", number) not in waited:
            waited.add(("own", number))
            own[number].wait()

    def product(unit, side):
        lhs = left[UNIT_LEFT[unit], :, side].reshape(4 * rows, 2 * tokens)
        return nn(lhs, right[unit])

    def first(unit):
        number = UNIT_LEFT[unit]
        own_ready(number)
        once(("left", number), [x_left[number]])
        once(("right", unit), [x_right[unit]])
        y_send[unit] = product(unit, 1 - y).astype(BF16).reshape(4, rows, width)
        y_copy[unit].start()

    far_end = jnp.where(lower, 3, 0)
    far_mid = jnp.where(lower, 2, 1)
    near_mid = jnp.where(lower, 1, 2)
    near_end = jnp.where(lower, 0, 3)

    def z_copy(unit, dest, peer, final_inside):
        target = inward.at[unit] if final_inside else passing.at[unit, dest]
        slot = 4 if final_inside else dest
        return remote(
            totals.at[unit, dest],
            target,
            z_send_sem.at[unit, dest],
            z_recv_sem.at[unit, slot],
            peer,
        )

    def add_passing(unit, dest):
        totals[unit, dest] = (
            totals[unit, dest].astype(F32) + passing[unit, dest].astype(F32)
        ).astype(BF16)

    def second(unit):
        if unit >= UNITS:
            own_ready(3)
            once("four", four_left + four_right)
            piece = slice((unit - UNITS) * rows, (unit - UNITS + 1) * rows)
            lhs = left_four[:, piece, :].reshape(4 * rows, 4 * tokens)
            out = nn(lhs, right_four[...])
        else:
            out = product(unit, y)
            y_copy[unit].wait_recv()
            out = out + y_recv[unit].reshape(4 * rows, width).astype(F32)
        totals[unit] = out.astype(BF16).reshape(4, rows, width)

        @pl.when(at_end)
        def _():
            z_copy(unit, far_end, in_peer, False).start()
            z_copy(unit, far_mid, in_peer, False).start()
            z_copy(unit, near_mid, in_peer, False).start()

    def third(unit):
        @pl.when(between)
        def _():
            z_copy(unit, far_end, in_peer, False).wait_recv()
            add_passing(unit, far_end)
            z_copy(unit, far_end, in_peer, False).start()
            z_copy(unit, far_mid, in_peer, False).wait_recv()
            add_passing(unit, far_mid)
            z_copy(unit, far_mid, in_peer, True).start()

    def fourth(unit):
        @pl.when(between)
        def _():
            z_copy(unit, near_end, out_peer, False).wait_recv()
            add_passing(unit, near_end)
            z_copy(unit, near_end, out_peer, True).start()

    def fifth(unit):
        z_copy(unit, z, in_peer, True).wait_recv()
        value = totals[unit, z].astype(F32) + inward[unit].astype(F32)

        @pl.when(at_end)
        def _():
            g_all[unit] = value

        @pl.when(between)
        def _():
            z_copy(unit, z, in_peer, False).wait_recv()
            g_all[unit] = value + passing[unit, z].astype(F32)

    def small_step(step):
        small_copy[step].wait_recv()
        total = small_own[step] + small_recv[step]
        if step < 3:
            small_own[step + 1] = total
            small_copy[step + 1].start()
        else:
            small_sum[...] = total

    class Sending:
        def greet(self, other):
            pl.semaphore_signal(barrier, inc=1, device_id=other, device_id_type=MESH)
            for peer in (x_peer, y_peer, xy_peer, in_peer, far_peer):
                pl.semaphore_signal(
                    barrier, inc=1, device_id=(section, peer), device_id_type=MESH
                )

            @pl.when(between)
            def _():
                pl.semaphore_signal(
                    barrier, inc=1, device_id=(section, out_peer), device_id_type=MESH
                )

        def met(self):
            @pl.when(at_end)
            def _():
                pl.semaphore_wait(barrier, 6)

            @pl.when(between)
            def _():
                pl.semaphore_wait(barrier, 7)

        def forward_done(self):
            start(own)
            start([four_left[1], x_left[0], four_left[2], four_left[0], x_left[2], x_left[1]])

        def branch_done(self):
            start([four_right[1], four_right[2], four_right[0]])

        def hidden_done(self, part):
            x_right[part].start()

        def attention_out_done(self):
            x_right[7].start()

        def attention_next(self):
            for unit in EARLY[0]:
                first(unit)

        def qkv_done(self):
            start(x_right[4:7])
            for unit in EARLY[1]:
                first(unit)

        def small_done(self):
            small_copy[0].start()

    block_body(
        Sending(),
        at_small,
        at_active,
        lambda k: right.at[k, 0:tokens] if k < UNITS else right_four.at[0:tokens],
        *given,
        activation,
        grad_in,
        small_own.at[0],
        *block_scratches,
    )

    stages = ((second, 0), (third, DEPTHS[0]), (fourth, DEPTHS[1]), (fifth, DEPTHS[2]))
    for turn in range(len(SECOND_ORDER) + DEPTHS[2]):
        if turn < len(FIRST_ORDER):
            first(FIRST_ORDER[turn])
        for stage, depth in stages:
            if 0 <= turn - depth < len(SECOND_ORDER):
                stage(SECOND_ORDER[turn - depth])
        if turn < 4:
            small_step(turn)

    for copy in four_left + four_right + x_left + x_right + y_copy + small_copy:
        copy.wait_send()

    @pl.when(at_end)
    def _():
        for unit in SECOND_ORDER:
            z_copy(unit, far_end, in_peer, False).wait_send()
            z_copy(unit, far_mid, in_peer, False).wait_send()
            z_copy(unit, near_mid, in_peer, False).wait_send()

    @pl.when(between)
    def _():
        for unit in SECOND_ORDER:
            z_copy(unit, far_end, in_peer, False).wait_send()
            z_copy(unit, far_mid, in_peer, True).wait_send()
            z_copy(unit, near_end, out_peer, True).wait_send()


def finish_kernel(
    activation,
    grad_in,
    g_all,
    small,
    activation_out,
    grad_in_out,
    g_qkv,
    g_out,
    g_fc1,
    g_fc2,
    g_gains,
    g_biases,
    g_fc1_bias,
    g_table,
    small_here,
    sems,
):
    rows, width = g_all.shape[1:]
    pairs = [(small, small_here), (activation, activation_out), (grad_in, grad_in_out)]
    for unit in range(UNITS + FOUR_UNITS):
        if unit < 4:
            target = g_fc1.at[:, unit * width : (unit + 1) * width]
        elif unit < 7:
            target = g_qkv.at[:, (unit - 4) * width : (unit - 3) * width]
        elif unit == 7:
            target = g_out
        else:
            target = g_fc2.at[(unit - UNITS) * rows : (unit - UNITS + 1) * rows, :]
        pairs.append((g_all.at[unit], target))
    copies = [
        pltpu.make_async_copy(source, target, sems.at[index])
        for index, (source, target) in enumerate(pairs)
    ]
    for copy in copies:
        copy.start()
    copies[0].wait()
    g_gains[...] = small_here[0:4, :]
    for row in range(g_biases.shape[0]):
        g_biases[row] = small_here[4 + row : 5 + row, :]
    for part in range(4):
        g_fc1_bias[0:1, part * width : (part + 1) * width] = small_here[10 + part : 11 + part, :]
    for head in range(g_table.shape[0]):
        g_table[head] = small_here[16 + head : 17 + head, 0 : g_table.shape[2]]
    for copy in copies[1:]:
        copy.wait()


def run_whole(inputs, cotangent, seg, wid, weights):
    w_qkv, w_out, w_fc1, w_fc2, gains, biases, fc1_bias, table = weights
    tokens, width = inputs.shape
    ff = w_fc1.shape[2]
    heads, rels = table.shape[1:]
    rows = width // 16
    all_units = UNITS + FOUR_UNITS
    whole = pl.BlockSpec(memory_space=pltpu.VMEM)
    anywhere = pl.BlockSpec(memory_space=pl.ANY)
    vm = pltpu.VMEM
    dma = pltpu.SemaphoreType.DMA
    activation, grad_in, g_all, small = pl.pallas_call(
        whole_kernel,
        out_shape=(
            jax.ShapeDtypeStruct((tokens, width), BF16),
            jax.ShapeDtypeStruct((tokens, width), F32),
            jax.ShapeDtypeStruct((all_units, rows, width), F32),
            jax.ShapeDtypeStruct((32, width), F32),
        ),
        in_specs=block_specs(),
        out_specs=(whole,) * 4,
        scratch_shapes=block_scratch(tokens, width, ff, heads, rels)
        + [
            vm((3, 4, 2, 2, rows, tokens), BF16),
            vm((4, 2, 2, ff // 16, tokens), BF16),
            vm((3, 4, 2, rows, 2 * tokens), BF16),
            vm((UNITS, 2 * tokens, width), BF16),
            vm((4, ff // 16, 4 * tokens), BF16),
            vm((4 * tokens, width), BF16),
            vm((UNITS, 4, rows, width), BF16),
            vm((UNITS, 4, rows, width), BF16),
            vm((all_units, 4, rows, width), BF16),
            vm((all_units, 4, rows, width), BF16),
            vm((all_units, rows, width), BF16),
            vm((4, 32, width), F32),
            vm((4, 32, width), F32),
            dma((4,)),
            dma((UNITS + 3,)),
            dma((UNITS + 3,)),
            dma((UNITS,)),
            dma((UNITS,)),
            dma((2, 4)),
            dma((2, 4)),
            dma((all_units, 4)),
            dma((all_units, 5)),
            dma((4,)),
            dma((4,)),
        ],
        compiler_params=pltpu.CompilerParams(
            collective_id=0, has_side_effects=True, vmem_limit_bytes=60 * 2**20
        ),
        name="whole",
    )(
        inputs,
        cotangent,
        seg,
        wid,
        w_qkv,
        w_out,
        w_fc1,
        w_fc2,
        gains,
        jnp.swapaxes(biases, 0, 1),
        fc1_bias,
        jnp.swapaxes(table, 0, 1),
    )
    activation, grad_in, g_qkv, g_out, g_fc1, g_fc2, g_gains, g_biases, g_fc1_bias, g_table = (
        pl.pallas_call(
            finish_kernel,
            out_shape=(
                jax.ShapeDtypeStruct((tokens, width), BF16),
                jax.ShapeDtypeStruct((tokens, width), F32),
                jax.ShapeDtypeStruct((rows, 3 * width), F32),
                jax.ShapeDtypeStruct((rows, width), F32),
                jax.ShapeDtypeStruct((rows, ff), F32),
                jax.ShapeDtypeStruct((ff // 16, width), F32),
                jax.ShapeDtypeStruct((4, width), F32),
                jax.ShapeDtypeStruct((6, 1, width), F32),
                jax.ShapeDtypeStruct((1, ff), F32),
                jax.ShapeDtypeStruct((heads, 1, rels), F32),
            ),
            in_specs=[anywhere] * 4,
            out_specs=(whole,) * 10,
            scratch_shapes=[vm((32, width), F32), dma((all_units + 3,))],
            compiler_params=pltpu.CompilerParams(vmem_limit_bytes=60 * 2**20),
            name="finish",
        )(activation, grad_in, g_all, small)
    )
    return (
        activation,
        grad_in,
        g_qkv[None],
        g_out[None],
        g_fc1[None],
        g_fc2[None],
        g_gains[None],
        jnp.swapaxes(g_biases, 0, 1),
        g_fc1_bias,
        jnp.swapaxes(g_table, 0, 1),
    )


def run_plain(inputs, cotangent, seg, wid, weights):
    w_qkv, w_out, w_fc1, w_fc2, gains, biases, fc1_bias, table = weights
    tokens, width = inputs.shape
    ff = w_fc1.shape[2]
    heads, rels = table.shape[1:]
    parts = ff // width
    whole = pl.BlockSpec(memory_space=pltpu.VMEM)
    activation, grad_in, at_small, at_active, b_all, small = pl.pallas_call(
        block_kernel,
        out_shape=(
            jax.ShapeDtypeStruct((tokens, width), BF16),
            jax.ShapeDtypeStruct((tokens, width), F32),
            jax.ShapeDtypeStruct((3, width, tokens), BF16),
            jax.ShapeDtypeStruct((parts, width, tokens), BF16),
            jax.ShapeDtypeStruct((parts + 5, tokens, width), BF16),
            jax.ShapeDtypeStruct((32, width), F32),
        ),
        in_specs=block_specs(),
        out_specs=(whole,) * 6,
        scratch_shapes=block_scratch(tokens, width, ff, heads, rels),
        compiler_params=pltpu.CompilerParams(
            collective_id=1, has_side_effects=True, vmem_limit_bytes=56 * 2**20
        ),
        name="block",
    )(
        inputs,
        cotangent,
        seg,
        wid,
        w_qkv,
        w_out,
        w_fc1,
        w_fc2,
        gains,
        jnp.swapaxes(biases, 0, 1),
        fc1_bias,
        jnp.swapaxes(table, 0, 1),
    )

    def scattered(left, right):
        grad = jnp.dot(left, right, preferred_element_type=F32)
        return lax.psum_scatter(grad, "batch", scatter_dimension=0, tiled=True)[None]

    def joined(first, count):
        return jnp.concatenate([b_all[first + number] for number in range(count)], axis=1)

    g_fc1 = scattered(at_small[0], joined(0, parts))
    g_qkv = scattered(at_small[1], joined(parts, 3))
    g_out = scattered(at_small[2], b_all[parts + 3])
    g_fc2 = scattered(at_active.reshape(ff, tokens), b_all[parts + 4])
    small = lax.psum(small, "batch")
    return (
        activation,
        grad_in,
        g_qkv,
        g_out,
        g_fc1,
        g_fc2,
        small[None, 0:4],
        small[None, 4:10],
        small[10:14].reshape(1, ff),
        small[None, 16 : 16 + heads, :rels],
    )


def per_device(
    inputs,
    cotangent,
    segments,
    row_widths,
    w_qkv,
    w_out,
    w_fc1,
    w_fc2,
    norm_gains,
    bias_rows,
    fc1_bias,
    rel_table,
):
    micro, _, slots, width = inputs.shape
    weights = (w_qkv, w_out, w_fc1, w_fc2, norm_gains, bias_rows, fc1_bias, rel_table)
    run = run_whole if lax.axis_size("batch") == 16 else run_plain
    activation, grad_in, *grads = run(
        inputs.reshape(micro * slots, width),
        cotangent.reshape(micro * slots, width),
        segments.reshape(micro, slots),
        row_widths.reshape(micro, row_widths.shape[2]),
        weights,
    )
    shape = (1, micro, 1, slots, width)
    return (activation.reshape(shape), grad_in.reshape(shape), *grads)


def solution(mesh):
    return jax.shard_map(
        per_device,
        mesh=mesh,
        in_specs=(
            P(None, "batch", None, None),
            P(None, "batch", None, None),
            P(None, "batch", None),
            P(None, "batch", None),
            P("section", None, None),
            P("section", None, None),
            P("section", None, None),
            P("section", None, None),
            P("section", None, None),
            P("section", None, None),
            P("section", None),
            P("section", None, None),
        ),
        out_specs=(
            P("section", None, "batch", None, None),
            P("section", None, "batch", None, None),
            P("section", "batch", None),
            P("section", "batch", None),
            P("section", "batch", None),
            P("section", "batch", None),
            P("section", None, None),
            P("section", None, None),
            P("section", None),
            P("section", None, None),
        ),
        check_vma=False,
    )
```

time: 166 us -> 131 us (0.79)
  Pallas kernels: 150 us -> 130 us
  local copies, waits for them, and re-layouts: 14.4 us -> 0 us
    pallas_call x2, Pallas kernels: 150 us -> 130 us  [the longest x1 127 us: run_whole(): pl.pallas_call(whole_kernel, out_shape=(jax.ShapeDtypeStruct((tokens, wid...]
    unnamed x22 -> x0, local copies, waits for them, and re-layouts: 14.4 us -> none
where the time goes in v3:
time: 131 us
  Pallas kernels  130 us (99%)
    pallas_call x1, Pallas kernels, run_whole(): pl.pallas_call(whole_kernel, out_shape=(jax.ShapeDtypeStruct((tokens, wid...  127 us
    pallas_call x1, Pallas kernels, run_whole(): pl.pallas_call(finish_kernel, out_shape=(jax.ShapeDtypeStruct((tokens, wi...  3.21 us

profile of v3, /device:TPU:0, one launch (start us, length us, event | category | flops | bytes accessed | tf_op | source)
XLA Modules:
  0.0 130.9 jit_solution(3087930456359597956)
XLA Ops:
  0.6 126.9 %whole.1 = (bf16[128,768]{1,0:T(8,128)(2,1)}, f32[128,768]{1,0:T(8,128)}, f32[12,48,768]{2,1,0:T(8,128)}, f32[32,768]{1,0:T(8,128)}) custom-call(bf16[128,768]{1,0:T(8,128)(2,1)} %bitcast.19, bf16[128,768]{1,0:T(8,128)(2,1)} %bitcast.20, s32[2,64]{1,0:T(2,128)} %bitcast.23, s32[2,4]{1,0:T(2,128)} %bitcast.24, bf16[1,768,2304]{2,1,0:T(8,128)(2,1)} %refs_4_.1, ...), custom_call_target="tpu_custom_call" | custom-call | tf_op jit(solution)/shard_map/whole/pallas_call | solution.py:959
  127.5 3.2 %finish.1 = (bf16[128,768]{1,0:T(8,128)(2,1)}, f32[128,768]{1,0:T(8,128)}, f32[48,2304]{1,0:T(8,128)}, f32[48,768]{1,0:T(8,128)}, f32[48,3072]{1,0:T(8,128)}, /*...) custom-call(bf16[128,768]{1,0:T(8,128)(2,1)} %get-tuple-element.24.a, ...), custom_call_target="tpu_custom_call" | custom-call | tf_op jit(solution)/shard_map/finish/pallas_call | solution.py:1015

commit v4 on v3

--- a/solution.py
+++ b/solution.py
@@ -288,6 +288,7 @@
 
     def turn_small(number, source):
         at_small[number] = source[...].T.reshape(at_small.shape[1:])
+        hooks.turned(number)
 
     hat, inv_scale = norm_parts(stream[...])
     hat_one[...] = hat
@@ -501,7 +502,7 @@
     def nothing(self, *_):
         pass
 
-    forward_done = branch_done = hidden_done = attention_out_done = nothing
+    turned = forward_done = branch_done = hidden_done = attention_out_done = nothing
     attention_next = qkv_done = small_done = nothing
 
 
@@ -571,10 +572,30 @@
 UNIT_LEFT = (0, 0, 0, 0, 1, 1, 1, 2)
 UNITS = len(UNIT_LEFT)
 FOUR_UNITS = 4
-EARLY = ((0, 1), (2, 3))
-FIRST_ORDER = (7, 4, 5, 6)
-SECOND_ORDER = (8, 9, 0, 1, 10, 2, 3, 11, 7, 4, 5, 6)
-DEPTHS = (2, 3, 5)
+AHEAD = 3
+FOUR_AT = 0
+
+
+def schedule(firsts, seconds, depths, small_at, started=0):
+    ops = []
+    for turn in range(started, len(seconds) + depths[2]):
+        if turn - started < len(firsts):
+            ops.append(f"x{firsts[turn - started]}")
+        for name, depth in zip("yzwe", (0,) + depths):
+            if max(0, started if depth == 0 else 0) <= turn - depth < len(seconds):
+                ops.append(f"{name}{seconds[turn - depth]}")
+        if turn == small_at:
+            ops.append("s")
+    for unit in seconds[: max(0, started - depths[0])]:
+        ops.insert(0, f"z{unit}")
+    return " ".join(ops + ["t"])
+
+
+OPS = (
+    "",
+    "y8 y9",
+    schedule((0, 1, 2, 3, 7, 4, 5, 6), (8, 9, 10, 11, 0, 1, 2, 3, 7, 4, 5, 6), (2, 3, 5), 12, 2),
+)
 
 
 def whole_kernel(*refs):
@@ -592,8 +613,10 @@
         totals,
         passing,
         inward,
-        small_own,
-        small_recv,
+        small,
+        small_parts,
+        small_in,
+        small_all,
         own_sem,
         x_send_sem,
         x_recv_sem,
@@ -603,8 +626,7 @@
         four_recv_sem,
         z_send_sem,
         z_recv_sem,
-        small_send_sem,
-        small_recv_sem,
+        small_sem,
     ) = rest[N_BLOCK_SCRATCH:]
     section = lax.axis_index("section")
     place = lax.axis_index("batch")
@@ -619,8 +641,6 @@
     lower = z < 2
     in_peer = jnp.where(lower, place + 4, place - 4)
     out_peer = jnp.where(at_end, place, jnp.where(z == 1, place - 4, place + 4))
-    far_peer = jnp.where(lower, place + 8, place - 8)
-    pair_peer = jnp.where(z % 2 == 0, place + 4, place - 4)
     tokens = given[0].shape[0]
     rows = left.shape[3]
     width = right.shape[2]
@@ -690,15 +710,25 @@
         )
         for unit in range(UNITS)
     ]
-    small_copy = [
+    small_out = [
         remote(
-            small_own.at[step],
-            small_recv.at[step],
-            small_send_sem.at[step],
-            small_recv_sem.at[step],
-            peer,
-        )
-        for step, peer in enumerate((x_peer, y_peer, pair_peer, far_peer))
+            small_parts.at[place ^ step],
+            small_in.at[place],
+            small_sem.at[0, step],
+            small_sem.at[1, step],
+            place ^ step,
+        )
+        for step in range(1, 16)
+    ]
+    small_back = [
+        remote(
+            small_all.at[place],
+            small_all.at[place],
+            small_sem.at[2, step],
+            small_sem.at[3, step],
+            place ^ step,
+        )
+        for step in range(1, 16)
     ]
 
     def start(copies):
@@ -722,11 +752,21 @@
         lhs = left[UNIT_LEFT[unit], :, side].reshape(4 * rows, 2 * tokens)
         return nn(lhs, right[unit])
 
+    ready, sent, used = [], [], []
+
+    def issue(units):
+        ready.extend(units)
+        while len(sent) < len(ready) and len(sent) - len(used) < AHEAD:
+            x_right[ready[len(sent)]].start()
+            sent.append(ready[len(sent)])
+
     def first(unit):
         number = UNIT_LEFT[unit]
         own_ready(number)
         once(("left", number), [x_left[number]])
         once(("right", unit), [x_right[unit]])
+        used.append(unit)
+        issue([])
         y_send[unit] = product(unit, 1 - y).astype(BF16).reshape(4, rows, width)
         y_copy[unit].start()
 
@@ -800,62 +840,77 @@
             z_copy(unit, z, in_peer, False).wait_recv()
             g_all[unit] = value + passing[unit, z].astype(F32)
 
-    def small_step(step):
-        small_copy[step].wait_recv()
-        total = small_own[step] + small_recv[step]
-        if step < 3:
-            small_own[step + 1] = total
-            small_copy[step + 1].start()
-        else:
-            small_sum[...] = total
+    def small_first():
+        for index in range(16):
+            small_parts[index] = small[2 * index : 2 * index + 2, :]
+        start(small_out)
+
+    def small_second():
+        total = small_parts[place]
+        for step, copy in enumerate(small_out, 1):
+            copy.wait_recv()
+            total = total + small_in[place ^ step]
+        small_all[place] = total
+        start(small_back)
+
+    def small_third():
+        for copy in small_back:
+            copy.wait_recv()
+        for index in range(16):
+            small_sum[2 * index : 2 * index + 2, :] = small_all[index]
+
+    stages = {"x": first, "y": second, "z": third, "w": fourth, "e": fifth}
+
+    def run_ops(ops):
+        for op in ops.split():
+            if op == "s":
+                small_second()
+            elif op == "t":
+                small_third()
+            else:
+                stages[op[0]](int(op[1:]))
 
     class Sending:
         def greet(self, other):
             pl.semaphore_signal(barrier, inc=1, device_id=other, device_id_type=MESH)
-            for peer in (x_peer, y_peer, xy_peer, in_peer, far_peer):
+            for step in range(1, 16):
                 pl.semaphore_signal(
-                    barrier, inc=1, device_id=(section, peer), device_id_type=MESH
+                    barrier, inc=1, device_id=(section, place ^ step), device_id_type=MESH
                 )
 
-            @pl.when(between)
-            def _():
-                pl.semaphore_signal(
-                    barrier, inc=1, device_id=(section, out_peer), device_id_type=MESH
-                )
-
         def met(self):
-            @pl.when(at_end)
-            def _():
-                pl.semaphore_wait(barrier, 6)
-
-            @pl.when(between)
-            def _():
-                pl.semaphore_wait(barrier, 7)
+            pl.semaphore_wait(barrier, 16)
+
+        def turned(self, number):
+            own[number].start()
+            x_left[number].start()
 
         def forward_done(self):
-            start(own)
-            start([four_left[1], x_left[0], four_left[2], four_left[0], x_left[2], x_left[1]])
+            own[3].start()
+            start(four_left)
 
         def branch_done(self):
-            start([four_right[1], four_right[2], four_right[0]])
+            start([four_right[1]])
+            if FOUR_AT == 0:
+                start([four_right[0], four_right[2]])
 
         def hidden_done(self, part):
-            x_right[part].start()
+            issue([part])
+            if part == 1 and FOUR_AT == 1:
+                start([four_right[0], four_right[2]])
 
         def attention_out_done(self):
-            x_right[7].start()
+            issue([7])
 
         def attention_next(self):
-            for unit in EARLY[0]:
-                first(unit)
+            run_ops(OPS[0])
 
         def qkv_done(self):
-            start(x_right[4:7])
-            for unit in EARLY[1]:
-                first(unit)
+            issue([4, 5, 6])
+            run_ops(OPS[1])
 
         def small_done(self):
-            small_copy[0].start()
+            small_first()
 
     block_body(
         Sending(),
@@ -865,33 +920,25 @@
         *given,
         activation,
         grad_in,
-        small_own.at[0],
+        small,
         *block_scratches,
     )
 
-    stages = ((second, 0), (third, DEPTHS[0]), (fourth, DEPTHS[1]), (fifth, DEPTHS[2]))
-    for turn in range(len(SECOND_ORDER) + DEPTHS[2]):
-        if turn < len(FIRST_ORDER):
-            first(FIRST_ORDER[turn])
-        for stage, depth in stages:
-            if 0 <= turn - depth < len(SECOND_ORDER):
-                stage(SECOND_ORDER[turn - depth])
-        if turn < 4:
-            small_step(turn)
-
-    for copy in four_left + four_right + x_left + x_right + y_copy + small_copy:
+    run_ops(OPS[2])
+
+    for copy in four_left + four_right + x_left + x_right + y_copy + small_out + small_back:
         copy.wait_send()
 
     @pl.when(at_end)
     def _():
-        for unit in SECOND_ORDER:
+        for unit in range(UNITS + FOUR_UNITS):
             z_copy(unit, far_end, in_peer, False).wait_send()
             z_copy(unit, far_mid, in_peer, False).wait_send()
             z_copy(unit, near_mid, in_peer, False).wait_send()
 
     @pl.when(between)
     def _():
-        for unit in SECOND_ORDER:
+        for unit in range(UNITS + FOUR_UNITS):
             z_copy(unit, far_end, in_peer, False).wait_send()
             z_copy(unit, far_mid, in_peer, True).wait_send()
             z_copy(unit, near_end, out_peer, True).wait_send()
@@ -979,8 +1026,10 @@
             vm((all_units, 4, rows, width), BF16),
             vm((all_units, 4, rows, width), BF16),
             vm((all_units, rows, width), BF16),
-            vm((4, 32, width), F32),
-            vm((4, 32, width), F32),
+            vm((32, width), F32),
+            vm((16, 2, width), F32),
+            vm((16, 2, width), F32),
+            vm((16, 2, width), F32),
             dma((4,)),
             dma((UNITS + 3,)),
             dma((UNITS + 3,)),
@@ -990,8 +1039,7 @@
             dma((2, 4)),
             dma((all_units, 4)),
             dma((all_units, 5)),
-            dma((4,)),
-            dma((4,)),
+            dma((4, 16)),
         ],
         compiler_params=pltpu.CompilerParams(
             collective_id=0, has_side_effects=True, vmem_limit_bytes=60 * 2**20

time: 131 us -> 112 us (0.85)
  Pallas kernels: 130 us -> 111 us
    pallas_call x1, Pallas kernels: 127 us -> 108 us  [run_whole(): pl.pallas_call(whole_kernel, out_shape=(jax.ShapeDtypeStruct((tokens, wid...]
where the time goes in v4:
time: 112 us
  Pallas kernels  111 us (99%)
    pallas_call x1, Pallas kernels, run_whole(): pl.pallas_call(whole_kernel, out_shape=(jax.ShapeDtypeStruct((tokens, wid...  108 us
    pallas_call x1, Pallas kernels, run_whole(): pl.pallas_call(finish_kernel, out_shape=(jax.ShapeDtypeStruct((tokens, wi...  3.21 us

profile of v4, /device:TPU:0, one launch (start us, length us, event | category | flops | bytes accessed | tf_op | source)
XLA Modules:
  0.0 112.2 jit_solution(2339738035700072972)
XLA Ops:
  0.6 108.2 %whole.1 = (bf16[128,768]{1,0:T(8,128)(2,1)}, f32[128,768]{1,0:T(8,128)}, f32[12,48,768]{2,1,0:T(8,128)}, f32[32,768]{1,0:T(8,128)}) custom-call(bf16[128,768]{1,0:T(8,128)(2,1)} %bitcast.19, bf16[128,768]{1,0:T(8,128)(2,1)} %bitcast.20, s32[2,64]{1,0:T(2,128)} %bitcast.23, s32[2,4]{1,0:T(2,128)} %bitcast.24, bf16[1,768,2304]{2,1,0:T(8,128)(2,1)} %refs_4_.1, ...), custom_call_target="tpu_custom_call" | custom-call | tf_op jit(solution)/shard_map/whole/pallas_call | solution.py:1006
  108.8 3.2 %finish.1 = (bf16[128,768]{1,0:T(8,128)(2,1)}, f32[128,768]{1,0:T(8,128)}, f32[48,2304]{1,0:T(8,128)}, f32[48,768]{1,0:T(8,128)}, f32[48,3072]{1,0:T(8,128)}, /*...) custom-call(bf16[128,768]{1,0:T(8,128)(2,1)} %get-tuple-element.24.a, ...), custom_call_target="tpu_custom_call" | custom-call | tf_op jit(solution)/shard_map/finish/pallas_call | solution.py:1063

commit v5 on v4

--- a/solution.py
+++ b/solution.py
@@ -174,8 +174,6 @@
 
 def block_body(
     hooks,
-    at_small,
-    at_active,
     b_at,
     inputs,
     cotangent,
@@ -287,8 +285,7 @@
         stream[...] = arrived[...].astype(F32)
 
     def turn_small(number, source):
-        at_small[number] = source[...].T.reshape(at_small.shape[1:])
-        hooks.turned(number)
+        hooks.turned(number, source[...].T)
 
     hat, inv_scale = norm_parts(stream[...])
     hat_one[...] = hat
@@ -356,7 +353,7 @@
         slope[:, at] = cumul + hidden * density
         if (index + 1) % per_part == 0:
             part = index // per_part
-            at_active[part] = active[:, cols_of(part, width)].T.reshape(at_active.shape[1:])
+            hooks.active_turned(part, active[:, cols_of(part, width)].T)
 
     for index in range(ff // COLS):
         feed(index)
@@ -491,6 +488,15 @@
 
 
 class Alone:
+    def __init__(self, at_small, at_active):
+        self.at_small, self.at_active = at_small, at_active
+
+    def turned(self, number, value):
+        self.at_small[number] = value
+
+    def active_turned(self, part, value):
+        self.at_active[part] = value
+
     def greet(self, other):
         pl.semaphore_signal(
             pltpu.get_barrier_semaphore(), inc=1, device_id=other, device_id_type=MESH
@@ -502,7 +508,7 @@
     def nothing(self, *_):
         pass
 
-    turned = forward_done = branch_done = hidden_done = attention_out_done = nothing
+    forward_done = branch_done = hidden_done = attention_out_done = nothing
     attention_next = qkv_done = small_done = nothing
 
 
@@ -513,7 +519,13 @@
         refs[18:],
     )
     block_body(
-        Alone(), at_small, at_active, lambda k: b_all.at[k], *given, activation, grad_in, small, *rest
+        Alone(at_small, at_active),
+        lambda k: b_all.at[k],
+        *given,
+        activation,
+        grad_in,
+        small,
+        *rest,
     )
 
 
@@ -572,7 +584,8 @@
 UNIT_LEFT = (0, 0, 0, 0, 1, 1, 1, 2)
 UNITS = len(UNIT_LEFT)
 FOUR_UNITS = 4
-AHEAD = 3
+SWAPPED = (1,)
+AHEAD = 8
 FOUR_AT = 0
 
 
@@ -594,7 +607,7 @@
 OPS = (
     "",
     "y8 y9",
-    schedule((0, 1, 2, 3, 7, 4, 5, 6), (8, 9, 10, 11, 0, 1, 2, 3, 7, 4, 5, 6), (2, 3, 5), 12, 2),
+    schedule((0, 1, 2, 4, 3, 5, 7, 6), (8, 9, 10, 11, 0, 1, 2, 4, 3, 5, 7, 6), (2, 3, 5), 12, 2),
 )
 
 
@@ -617,7 +630,6 @@
         small_parts,
         small_in,
         small_all,
-        own_sem,
         x_send_sem,
         x_recv_sem,
         y_send_sem,
@@ -656,18 +668,11 @@
             device_id_type=MESH,
         )
 
-    own = [
-        pltpu.make_async_copy(
-            at_small.at[number, :, :, x], left.at[number, :, :, :, 0:tokens], own_sem.at[number]
-        )
-        for number in range(3)
-    ] + [pltpu.make_async_copy(at_active.at[:, y, x], left_four.at[:, :, 0:tokens], own_sem.at[3])]
-
     others = ((1, y, 1 - x, x_peer), (2, 1 - y, x, y_peer), (3, 1 - y, 1 - x, xy_peer))
     four_left = [
         remote(
-            at_active.at[:, peer_y, peer_x],
-            left_four.at[:, :, slot * tokens : (slot + 1) * tokens],
+            at_active.at[peer_y, peer_x],
+            left_four.at[slot - 1],
             four_send_sem.at[0, slot],
             four_recv_sem.at[0, slot],
             peer,
@@ -686,11 +691,11 @@
     ]
     x_left = [
         remote(
-            at_small.at[number, :, :, 1 - x],
-            left.at[number, :, :, :, tokens : 2 * tokens],
+            at_small.at[number, 1 - (y if number in SWAPPED else x)],
+            left.at[number],
             x_send_sem.at[UNITS + number],
             x_recv_sem.at[UNITS + number],
-            x_peer,
+            y_peer if number in SWAPPED else x_peer,
         )
         for number in range(3)
     ]
@@ -700,13 +705,17 @@
             right.at[unit, tokens : 2 * tokens, :],
             x_send_sem.at[unit],
             x_recv_sem.at[unit],
-            x_peer,
+            y_peer if UNIT_LEFT[unit] in SWAPPED else x_peer,
         )
         for unit in range(UNITS)
     ]
     y_copy = [
         remote(
-            y_send.at[unit], y_recv.at[unit], y_send_sem.at[unit], y_recv_sem.at[unit], y_peer
+            y_send.at[unit],
+            y_recv.at[unit],
+            y_send_sem.at[unit],
+            y_recv_sem.at[unit],
+            x_peer if UNIT_LEFT[unit] in SWAPPED else y_peer,
         )
         for unit in range(UNITS)
     ]
@@ -743,14 +752,13 @@
             for copy in copies:
                 copy.wait_recv()
 
-    def own_ready(number):
-        if ("own", number) not in waited:
-            waited.add(("own", number))
-            own[number].wait()
-
-    def product(unit, side):
-        lhs = left[UNIT_LEFT[unit], :, side].reshape(4 * rows, 2 * tokens)
-        return nn(lhs, right[unit])
+    def product(unit, own):
+        number = UNIT_LEFT[unit]
+        held, side = (y, x) if number in SWAPPED else (x, y)
+        if not own:
+            side = 1 - side
+        lhs = jnp.concatenate([at_small[number, held, :, side], left[number, :, side]], axis=2)
+        return nn(lhs.reshape(4 * rows, 2 * tokens), right[unit])
 
     ready, sent, used = [], [], []
 
@@ -762,12 +770,11 @@
 
     def first(unit):
         number = UNIT_LEFT[unit]
-        own_ready(number)
         once(("left", number), [x_left[number]])
         once(("right", unit), [x_right[unit]])
         used.append(unit)
         issue([])
-        y_send[unit] = product(unit, 1 - y).astype(BF16).reshape(4, rows, width)
+        y_send[unit] = product(unit, False).astype(BF16).reshape(4, rows, width)
         y_copy[unit].start()
 
     far_end = jnp.where(lower, 3, 0)
@@ -793,13 +800,15 @@
 
     def second(unit):
         if unit >= UNITS:
-            own_ready(3)
             once("four", four_left + four_right)
             piece = slice((unit - UNITS) * rows, (unit - UNITS + 1) * rows)
-            lhs = left_four[:, piece, :].reshape(4 * rows, 4 * tokens)
-            out = nn(lhs, right_four[...])
+            lhs = jnp.concatenate(
+                [at_active[y, x, :, piece, :]] + [left_four[slot, :, piece, :] for slot in range(3)],
+                axis=2,
+            )
+            out = nn(lhs.reshape(4 * rows, 4 * tokens), right_four[...])
         else:
-            out = product(unit, y)
+            out = product(unit, True)
             y_copy[unit].wait_recv()
             out = out + y_recv[unit].reshape(4 * rows, width).astype(F32)
         totals[unit] = out.astype(BF16).reshape(4, rows, width)
@@ -881,12 +890,21 @@
         def met(self):
             pl.semaphore_wait(barrier, 16)
 
-        def turned(self, number):
-            own[number].start()
+        def turned(self, number, value):
+            shares = value.reshape(4, 2, 2, rows, tokens)
+            for side in range(2):
+                at_small[number, side] = (
+                    shares[:, side] if number in SWAPPED else shares[:, :, side]
+                )
             x_left[number].start()
 
+        def active_turned(self, part, value):
+            shares = value.reshape(2, 2, left_four.shape[2], tokens)
+            for high in range(2):
+                for side in range(2):
+                    at_active[high, side, part] = shares[high, side]
+
         def forward_done(self):
-            own[3].start()
             start(four_left)
 
         def branch_done(self):
@@ -914,8 +932,6 @@
 
     block_body(
         Sending(),
-        at_small,
-        at_active,
         lambda k: right.at[k, 0:tokens] if k < UNITS else right_four.at[0:tokens],
         *given,
         activation,
@@ -1015,11 +1031,11 @@
         out_specs=(whole,) * 4,
         scratch_shapes=block_scratch(tokens, width, ff, heads, rels)
         + [
-            vm((3, 4, 2, 2, rows, tokens), BF16),
-            vm((4, 2, 2, ff // 16, tokens), BF16),
-            vm((3, 4, 2, rows, 2 * tokens), BF16),
+            vm((3, 2, 4, 2, rows, tokens), BF16),
+            vm((2, 2, 4, ff // 16, tokens), BF16),
+            vm((3, 4, 2, rows, tokens), BF16),
             vm((UNITS, 2 * tokens, width), BF16),
-            vm((4, ff // 16, 4 * tokens), BF16),
+            vm((3, 4, ff // 16, tokens), BF16),
             vm((4 * tokens, width), BF16),
             vm((UNITS, 4, rows, width), BF16),
             vm((UNITS, 4, rows, width), BF16),
@@ -1030,7 +1046,6 @@
             vm((16, 2, width), F32),
             vm((16, 2, width), F32),
             vm((16, 2, width), F32),
-            dma((4,)),
             dma((UNITS + 3,)),
             dma((UNITS + 3,)),
             dma((UNITS,)),

time: 112 us -> 110 us (0.982)
  Pallas kernels: 111 us -> 109 us
    pallas_call x1, Pallas kernels: 108 us -> 105 us  [run_whole(): pl.pallas_call(whole_kernel, out_shape=(jax.ShapeDtypeStruct((tokens, wid...]
where the time goes in v5:
time: 110 us; the launch traced here: 109 us
  Pallas kernels  109 us (99%)
    pallas_call x1, Pallas kernels, run_whole(): pl.pallas_call(whole_kernel, out_shape=(jax.ShapeDtypeStruct((tokens, wid...  105 us
    pallas_call x1, Pallas kernels, run_whole(): pl.pallas_call(finish_kernel, out_shape=(jax.ShapeDtypeStruct((tokens, wi...  3.21 us

profile of v5, /device:TPU:0, one launch (start us, length us, event | category | flops | bytes accessed | tf_op | source)
XLA Modules:
  0.0 109.4 jit_solution(9217211859604708684)
XLA Ops:
  0.6 105.4 %whole.1 = (bf16[128,768]{1,0:T(8,128)(2,1)}, f32[128,768]{1,0:T(8,128)}, f32[12,48,768]{2,1,0:T(8,128)}, f32[32,768]{1,0:T(8,128)}) custom-call(bf16[128,768]{1,0:T(8,128)(2,1)} %bitcast.19, bf16[128,768]{1,0:T(8,128)(2,1)} %bitcast.20, s32[2,64]{1,0:T(2,128)} %bitcast.23, s32[2,4]{1,0:T(2,128)} %bitcast.24, bf16[1,768,2304]{2,1,0:T(8,128)(2,1)} %refs_4_.1, ...), custom_call_target="tpu_custom_call" | custom-call | tf_op jit(solution)/shard_map/whole/pallas_call | solution.py:1022
  106.1 3.2 %finish.1 = (bf16[128,768]{1,0:T(8,128)(2,1)}, f32[128,768]{1,0:T(8,128)}, f32[48,2304]{1,0:T(8,128)}, f32[48,768]{1,0:T(8,128)}, f32[48,3072]{1,0:T(8,128)}, /*...) custom-call(bf16[128,768]{1,0:T(8,128)(2,1)} %get-tuple-element.24.a, ...), custom_call_target="tpu_custom_call" | custom-call | tf_op jit(solution)/shard_map/finish/pallas_call | solution.py:1078

commit v6 on v5

--- a/solution.py
+++ b/solution.py
@@ -905,7 +905,7 @@
                     at_active[high, side, part] = shares[high, side]
 
         def forward_done(self):
-            start(four_left)
+            start([four_left[1], four_left[0], four_left[2]])
 
         def branch_done(self):
             start([four_right[1]])

time: 110 us -> 110 us (level)
  no operation moved by 1% of the time
where the time goes in v6:
time: 110 us; the launch traced here: 109 us
  Pallas kernels  109 us (99%)
    pallas_call x1, Pallas kernels, run_whole(): pl.pallas_call(whole_kernel, out_shape=(jax.ShapeDtypeStruct((tokens, wid...  105 us
    pallas_call x1, Pallas kernels, run_whole(): pl.pallas_call(finish_kernel, out_shape=(jax.ShapeDtypeStruct((tokens, wi...  3.21 us

profile of v6, /device:TPU:0, one launch (start us, length us, event | category | flops | bytes accessed | tf_op | source)
XLA Modules:
  0.0 109.4 jit_solution(4778803975085174520)
XLA Ops:
  0.6 105.4 %whole.1 = (bf16[128,768]{1,0:T(8,128)(2,1)}, f32[128,768]{1,0:T(8,128)}, f32[12,48,768]{2,1,0:T(8,128)}, f32[32,768]{1,0:T(8,128)}) custom-call(bf16[128,768]{1,0:T(8,128)(2,1)} %bitcast.19, bf16[128,768]{1,0:T(8,128)(2,1)} %bitcast.20, s32[2,64]{1,0:T(2,128)} %bitcast.23, s32[2,4]{1,0:T(2,128)} %bitcast.24, bf16[1,768,2304]{2,1,0:T(8,128)(2,1)} %refs_4_.1, ...), custom_call_target="tpu_custom_call" | custom-call | tf_op jit(solution)/shard_map/whole/pallas_call | solution.py:1022
  106.1 3.2 %finish.1 = (bf16[128,768]{1,0:T(8,128)(2,1)}, f32[128,768]{1,0:T(8,128)}, f32[48,2304]{1,0:T(8,128)}, f32[48,768]{1,0:T(8,128)}, f32[48,3072]{1,0:T(8,128)}, /*...) custom-call(bf16[128,768]{1,0:T(8,128)(2,1)} %get-tuple-element.24.a, ...), custom_call_target="tpu_custom_call" | custom-call | tf_op jit(solution)/shard_map/finish/pallas_call | solution.py:1078
